TPU v7x, 512 devices: a whole 4x8x8 slice. The times are simulated.
512 devices in a mesh: dp: 64 (over x, y_lo, z), ctx: 8 (over y_hi, core).
Axes of the slice: x: 4, y: 8 (y_hi: 4, y_lo: 2; y = y_hi * 2 + y_lo), z: 8, core: 2. Of those that a mesh axis runs over, the one named last changes fastest.
Arguments:
- query_in: bfloat16 [64, 1024, 1024], P('dp', 'ctx'), may hold values from -6 to 6
- key_in: bfloat16 [64, 1024, 1024], P('dp', 'ctx'), may hold values from -6 to 6
- value_in: bfloat16 [64, 1024, 1024], P('dp', 'ctx'), may hold values from -6 to 6
- gate_in: bfloat16 [64, 1024, 1024], P('dp', 'ctx'), may hold values from -6 to 6
- out_grad: bfloat16 [64, 1024, 1024], P('dp', 'ctx'), may hold values from -6 to 6
- out_weight: bfloat16 [1024, 1024], P('dp'), may hold values from -0.1875 to 0.1875
- lengths: int32 [64, 8], P('dp'), may hold values from 1 to 512, 1024 in all within a row
- stamps: int32 [64, 1024], P('dp'), may hold values from 1 to 6291456, as said below
- pos_bias: float32 [1024], replicated, may hold values from -3 to 3
- time_bias: float32 [32], replicated, may hold values from -3 to 3
Outputs:
- layer_out: bfloat16 [64, 1024, 1024], P('dp', 'ctx')
- query_grad: bfloat16 [64, 1024, 1024], P('dp', 'ctx')
- key_grad: bfloat16 [64, 1024, 1024], P('dp', 'ctx')
- value_grad: bfloat16 [64, 1024, 1024], P('dp', 'ctx')
- gate_grad: bfloat16 [64, 1024, 1024], P('dp', 'ctx')
- weight_grad: float32 [1024, 1024], P('dp')
- pos_grad: float32 [1024], replicated
- time_grad: float32 [32], replicated
Inputs may be any that keep to these rules, and one draw needn't show every extreme that they name: In every pack the 8 lengths add up to 1024 and the longest is exactly 512. `stamps`: timestamps rise strictly along each pack; each pack's first is 1 and its last is 6291456.
All inputs are finite; a program needn't handle non-finite values.
Results may differ from a plain program's by a relative error of at most 0.015.
Values may be sent and summed in bfloat16 or wider, within the bound.
A program may use at most 64 MiB of HBM per device.

v0:
```python
import jax
import jax.numpy as jnp
from jax import lax
from jax.sharding import PartitionSpec as P

HEAD_DIM = 128


EPSILON = 1e-06


def bucket_of(time_gap):
    bucket = jnp.zeros(time_gap.shape, jnp.int32)
    for shift_by in range(31):
        bucket = bucket + (time_gap >= 1 << shift_by).astype(jnp.int32)
    return bucket


def toeplitz(table, offset, row_total, col_total):
    length = table.shape[0]
    extended = jnp.concatenate(
        [jnp.zeros((length + col_total,), table.dtype), table, jnp.zeros((row_total,), table.dtype)]
    )
    diag_span = row_total + col_total - 1
    window = lax.dynamic_slice_in_dim(extended, length + offset + 1, diag_span)
    flipped = window[::-1]
    repeated = jnp.tile(flipped, row_total + 1)[: row_total * (diag_span + 1)]
    sliding = repeated.reshape(row_total, diag_span + 1)[:, :col_total]
    return sliding[::-1]


def block_bias(pos_table, time_table, query_stamps, key_stamps, offset):
    row_total = query_stamps.shape[0]
    col_total = key_stamps.shape[0]
    bucket = bucket_of(jnp.abs(query_stamps[:, None] - key_stamps[None, :]))
    timed = jnp.zeros((row_total, col_total), jnp.float32)
    for bucket_no in range(time_table.shape[0]):
        timed = timed + jnp.where(bucket == bucket_no, time_table[bucket_no], 0.0)
    return toeplitz(pos_table, offset, row_total, col_total) + timed


def split_heads(block_rows):
    return block_rows.reshape(block_rows.shape[0], block_rows.shape[1] // HEAD_DIM, HEAD_DIM)


def score_grads(scores, pair_mask, grad_block, value_block):
    weight_grads = jnp.einsum(
        "rhd,chd->hrc",
        split_heads(grad_block),
        split_heads(value_block),
        preferred_element_type=jnp.float32,
    )
    gate_sig = jax.nn.sigmoid(scores)
    return jnp.where(
        pair_mask[None], weight_grads * gate_sig * (1.0 + scores * (1.0 - gate_sig)), 0.0
    )


def on_device(
    query_in, key_in, value_in, gate_in, out_grad, out_weight, lengths, stamps, pos_bias, time_bias
):
    query_mine = query_in[0]
    key_mine = key_in[0]
    value_mine = value_in[0]
    gate_mine = gate_in[0]
    grad_mine = out_grad[0]
    row_count = query_mine.shape[0]
    context = stamps.shape[1]
    stamp_row = stamps[0]
    user_ends = jnp.cumsum(lengths[0])
    places = lax.iota(jnp.int32, context)
    user_ids = jnp.sum((places[:, None] >= user_ends[None, :]).astype(jnp.int32), axis=1)
    my_first = lax.axis_index("ctx") * row_count
    factor = HEAD_DIM ** (-0.5)

    def pair_terms(query_block, key_block, query_first, key_first):
        query_size = query_block.shape[0]
        key_size = key_block.shape[0]
        query_users = lax.dynamic_slice_in_dim(user_ids, query_first, query_size)
        key_users = lax.dynamic_slice_in_dim(user_ids, key_first, key_size)
        query_stamps = lax.dynamic_slice_in_dim(stamp_row, query_first, query_size)
        key_stamps = lax.dynamic_slice_in_dim(stamp_row, key_first, key_size)
        query_places = query_first + lax.iota(jnp.int32, query_size)
        key_places = key_first + lax.iota(jnp.int32, key_size)
        pair_mask = (query_users[:, None] == key_users[None, :]) & (
            query_places[:, None] >= key_places[None, :]
        )

        def bias_of(table_pos, table_time):
            return block_bias(
                table_pos, table_time, query_stamps, key_stamps, query_first - key_first
            )

        pair_bias, pull_back = jax.vjp(bias_of, pos_bias, time_bias)
        scores = (
            jnp.einsum(
                "rhd,chd->hrc",
                split_heads(query_block),
                split_heads(key_block),
                preferred_element_type=jnp.float32,
            )
            * factor
            + pair_bias[None]
        )
        return (scores, pair_mask, pull_back)

    key_all, value_all = (
        lax.all_gather(key_mine, "ctx", axis=0, tiled=True),
        lax.all_gather(value_mine, "ctx", axis=0, tiled=True),
    )
    query_size = min(512, query_mine.shape[0])
    key_size = min(512, key_all.shape[0])
    col_count = query_mine.shape[1]

    def forward_per_query(query_step):
        query_start = my_first + query_step * query_size

        def forward_per_key(carried, key_step):
            key_start = 0 + key_step * key_size
            key_block = lax.dynamic_slice_in_dim(key_all, key_step * key_size, key_size)
            value_block = lax.dynamic_slice_in_dim(value_all, key_step * key_size, key_size)
            scores, pair_mask, pull_back = pair_terms(query_mine, key_block, query_start, key_start)
            weights = jnp.where(pair_mask[None], jax.nn.silu(scores), 0.0).astype(jnp.bfloat16)
            attended_part = jnp.einsum(
                "hrc,chd->rhd",
                weights,
                split_heads(value_block),
                preferred_element_type=jnp.float32,
            )
            return (carried + attended_part.reshape(query_size, col_count), None)

        zeros_init = jnp.zeros((query_size, col_count), jnp.float32)
        result, unused = lax.scan(
            forward_per_key, zeros_init, lax.iota(jnp.int32, key_all.shape[0] // key_size)
        )
        return result

    outputs = lax.map(forward_per_query, lax.iota(jnp.int32, query_mine.shape[0] // query_size))
    attended = outputs.reshape(query_mine.shape).astype(jnp.bfloat16)
    attended_wide = attended.astype(jnp.float32)
    center = attended_wide - jnp.mean(attended_wide, axis=1, keepdims=True)
    inv_dev = lax.rsqrt(jnp.mean(center * center, axis=1, keepdims=True) + EPSILON)
    normed = center * inv_dev
    gate_wide = gate_mine.astype(jnp.float32)
    mixed_rows = (normed * gate_wide).astype(jnp.bfloat16)
    contract_cols = (((1,), (1,)), ((), ()))
    whole_rows = lax.all_gather(out_weight, "dp", axis=0, tiled=True)
    layer_out = jnp.dot(mixed_rows, whole_rows, preferred_element_type=jnp.float32)
    mixed_grad = lax.dot_general(
        grad_mine, whole_rows, contract_cols, preferred_element_type=jnp.float32
    )
    weight_part = lax.psum_scatter(
        lax.dot_general(
            mixed_rows, grad_mine, (((0,), (0,)), ((), ())), preferred_element_type=jnp.float32
        ),
        "dp",
        scatter_dimension=0,
        tiled=True,
    )
    weight_grad = lax.psum(weight_part, "ctx")
    gate_grad = (mixed_grad * normed).astype(jnp.bfloat16)
    normed_grad = mixed_grad * gate_wide
    attn_grad = inv_dev * (
        normed_grad
        - jnp.mean(normed_grad, axis=1, keepdims=True)
        - normed * jnp.mean(normed_grad * normed, axis=1, keepdims=True)
    )
    attn_grad = attn_grad.astype(jnp.bfloat16)
    grad_rows = attn_grad
    query_query_size = min(512, query_mine.shape[0])
    query_key_size = min(512, key_all.shape[0])
    query_col_count = query_mine.shape[1]

    def query_per_query(query_step):
        query_start = my_first + query_step * query_query_size

        def query_per_key(carried, key_step):
            key_start = 0 + key_step * query_key_size
            key_block = lax.dynamic_slice_in_dim(key_all, key_step * query_key_size, query_key_size)
            value_block = lax.dynamic_slice_in_dim(
                value_all, key_step * query_key_size, query_key_size
            )
            scores, pair_mask, pull_back = pair_terms(query_mine, key_block, query_start, key_start)
            score_grad = score_grads(scores, pair_mask, grad_rows, value_block)
            pos_part, time_part = pull_back(jnp.sum(score_grad, axis=0))
            query_part = jnp.einsum(
                "hrc,chd->rhd",
                score_grad.astype(jnp.bfloat16),
                split_heads(key_block),
                preferred_element_type=jnp.float32,
            )
            return (
                (
                    carried[0] + query_part.reshape(query_query_size, query_col_count),
                    carried[1] + pos_part,
                    carried[2] + time_part,
                ),
                None,
            )

        zeros_init = (
            jnp.zeros((query_query_size, query_col_count), jnp.float32),
            jnp.zeros(pos_bias.shape, jnp.float32),
            jnp.zeros(time_bias.shape, jnp.float32),
        )
        result, unused = lax.scan(
            query_per_key, zeros_init, lax.iota(jnp.int32, key_all.shape[0] // query_key_size)
        )
        return result

    query_sums, pos_sums, time_sums = lax.map(
        query_per_query, lax.iota(jnp.int32, query_mine.shape[0] // query_query_size)
    )
    query_grad = (query_sums.reshape(query_mine.shape) * factor).astype(jnp.bfloat16)
    query_grad, pos_local, time_local = (
        query_grad,
        jnp.sum(pos_sums, axis=0),
        jnp.sum(time_sums, axis=0),
    )
    query_all, grad_all = (
        lax.all_gather(query_mine, "ctx", axis=0, tiled=True),
        lax.all_gather(attn_grad, "ctx", axis=0, tiled=True),
    )
    key_query_size = min(512, query_all.shape[0])
    key_key_size = min(512, key_mine.shape[0])
    key_col_count = key_mine.shape[1]

    def key_per_key(key_step):
        key_start = my_first + key_step * key_key_size

        def per_per_query(carried, query_step):
            query_start = 0 + query_step * key_query_size
            query_block = lax.dynamic_slice_in_dim(
                query_all, query_step * key_query_size, key_query_size
            )
            grad_block = lax.dynamic_slice_in_dim(
                grad_all, query_step * key_query_size, key_query_size
            )
            scores, pair_mask, pull_back = pair_terms(query_block, key_mine, query_start, key_start)
            weights = jnp.where(pair_mask[None], jax.nn.silu(scores), 0.0).astype(jnp.bfloat16)
            score_grad = score_grads(scores, pair_mask, grad_block, value_mine)
            value_part = jnp.einsum(
                "hrc,rhd->chd", weights, split_heads(grad_block), preferred_element_type=jnp.float32
            )
            key_part = jnp.einsum(
                "hrc,rhd->chd",
                score_grad.astype(jnp.bfloat16),
                split_heads(query_block),
                preferred_element_type=jnp.float32,
            )
            return (
                (
                    carried[0] + key_part.reshape(key_key_size, key_col_count),
                    carried[1] + value_part.reshape(key_key_size, key_col_count),
                ),
                None,
            )

        zero_rows = jnp.zeros((key_key_size, key_col_count), jnp.float32)
        result, unused = lax.scan(
            per_per_query,
            (zero_rows, zero_rows),
            lax.iota(jnp.int32, query_all.shape[0] // key_query_size),
        )
        return result

    key_sums, value_sums = lax.map(
        key_per_key, lax.iota(jnp.int32, key_mine.shape[0] // key_key_size)
    )
    key_grad = (key_sums.reshape(key_mine.shape) * factor).astype(jnp.bfloat16)
    key_grad, value_grad = (key_grad, value_sums.reshape(key_mine.shape).astype(jnp.bfloat16))
    pos_grad, time_grad = lax.psum((pos_local, time_local), ("dp", "ctx"))
    return (
        layer_out.astype(jnp.bfloat16)[None],
        query_grad[None],
        key_grad[None],
        value_grad[None],
        gate_grad[None],
        weight_grad,
        pos_grad,
        time_grad,
    )


def solution(mesh):
    placed = (
        P("dp", "ctx", None),
        P("dp", "ctx", None),
        P("dp", "ctx", None),
        P("dp", "ctx", None),
        P("dp", "ctx", None),
        P("dp", None),
        P("dp", None),
        P("dp", None),
        P(),
        P(),
    )
    return jax.shard_map(
        on_device,
        mesh=mesh,
        in_specs=placed,
        out_specs=(
            P("dp", "ctx", None),
            P("dp", "ctx", None),
            P("dp", "ctx", None),
            P("dp", "ctx", None),
            P("dp", "ctx", None),
            P("dp", None),
            P(),
            P(),
        ),
        check_vma=False,
    )
```

profile of v0, /device:TPU:1, one launch (start us, length us, event | category | flops | bytes accessed | tf_op | source)
XLA Modules:
  0.0 893.9 jit_solution(12226835931457690420)
XLA Ops:
  7.3 1.9 copy.112
  9.2 1.8 copy.113
  11.8 1.8 copy.116
  14.1 45.8 %all-gather.13.cloned.1.call-done = bf16[1,1024,1024]{1,2,0:T(8,128)(2,1)} async-done(((bf16[1,128,1024]{1,2,0:T(8,128)(2,1)}), bf16[1,1024,1024]{1,2,0:T(8,128)(2,1)}) %all-gather.13.cloned.1.call-update) | async-done | bytes 2097168 | tf_op jit(solution)/shard_map/all_gather | solution.py:109
  59.9 44.1 %all-gather.15.cloned.1.call-done = bf16[1,1024,1024]{1,2,0:T(8,128)(2,1)} async-done(((bf16[1,128,1024]{1,2,0:T(8,128)(2,1)}), bf16[1,1024,1024]{1,2,0:T(8,128)(2,1)}) %all-gather.15.cloned.1.call-update) | async-done | bytes 2097168 | tf_op jit(solution)/shard_map/all_gather | solution.py:108
  104.0 72.8 %while.78 = (s32[]{:T(128)}, f32[128,1024]{0,1:T(8,128)}, s32[2]{0:T(128)S(1)}, bf16[1024,1024]{0,1:T(8,128)(2,1)}, s32[128]{0:T(128)S(1)}, /*index=5*/s32[1024]...) while((s32[]{:T(128)}, f32[128,1024]{0,1:T(8,128)}, ...), condition=%wide.region_3.4_spmd.clone, body=%wide.region_2.3_spmd.clone.sunk | while | flops 285542272 | bytes 18211576 | solution.py:133
  105.3 1.7 constant_dynamic-slice_fusion.10
  108.5 1.7 rev.84
  111.7 21.8 %add_add_fusion.6 = f32[128,512]{1,0:T(8,128)S(1)} fusion(f32[128,512]{1,0:T(8,128)S(1)} %rev.84, f32[]{:T(128)} %bitcast.417, f32[]{:T(128)} %bitcast.418, f32[]{:T(128)} %bitcast.419, f32[]{:T(128)} %bitcast.420, f32[]{:T(128)} %bitcast.421, f32[]{:T(128)} %bitcast.422, f32[]{:T(128)} %bitcast.423, f32[]{:T(128)} %bitcast.424, f32[]{:T(128)} %bitcast.425, ...), kind=kLoop, calls=%fused_computation.10.clone.1 | loop fusion | flops 12451840 | bytes 526976 | tf_op jit(solution)/shard_map/while/body/eval_jaxpr/while/body/eval_jaxpr/jvp()/add | solution.py:39
  135.3 3.1 fusion.217
  141.7 1.7 constant_dynamic-slice_fusion.10
  144.9 1.7 rev.84
  148.1 21.8 %add_add_fusion.6 = f32[128,512]{1,0:T(8,128)S(1)} fusion(f32[128,512]{1,0:T(8,128)S(1)} %rev.84, f32[]{:T(128)} %bitcast.417, f32[]{:T(128)} %bitcast.418, f32[]{:T(128)} %bitcast.419, f32[]{:T(128)} %bitcast.420, f32[]{:T(128)} %bitcast.421, f32[]{:T(128)} %bitcast.422, f32[]{:T(128)} %bitcast.423, f32[]{:T(128)} %bitcast.424, f32[]{:T(128)} %bitcast.425, ...), kind=kLoop, calls=%fused_computation.10.clone.1 | loop fusion | flops 12451840 | bytes 526976 | tf_op jit(solution)/shard_map/while/body/eval_jaxpr/while/body/eval_jaxpr/jvp()/add | solution.py:39
  171.8 3.1 fusion.217
  178.4 184.6 %all-gather.9.cloned.1.call-done = bf16[1024,1024]{1,0:T(8,128)(2,1)} async-done(((bf16[16,1024]{1,0:T(8,128)(2,1)}), bf16[1024,1024]{1,0:T(8,128)(2,1)}) %all-gather.9.cloned.1.call-update) | async-done | bytes 2097168 | tf_op jit(solution)/shard_map/all_gather | solution.py:147
  363.0 2.5 fusion.156
  366.8 2.8 fusion.152
  371.1 150.5 %while.79 = (s32[]{:T(128)}, f32[128,1024]{0,1:T(8,128)}, f32[1024]{0:T(1024)S(1)}, f32[32]{0:T(128)S(1)}, s32[2]{0:T(128)S(1)}, /*index=5*/bf16[1024,1024]{0,1:...) while((s32[]{:T(128)}, f32[128,1024]{0,1:T(8,128)}, ...), condition=%wide.region_43.44_spmd.clone, body=%wide.region_8.43_spmd.clone.sunk | while | flops 434852608 | bytes 32417576 | solution.py:206
  372.4 2.5 constant_dynamic-slice_fusion.11
  375.9 2.1 tile.78
  377.9 1.7 slice.1302
  379.6 1.8 reshape.483
  381.4 1.7 slice.1303
  383.1 1.8 copy.169
  384.9 3.1 rev.85
  389.5 22.5 %add_add_fusion.7 = f32[128,512]{0,1:T(8,128)S(1)} fusion(f32[128,512]{0,1:T(8,128)} %rev.85, f32[]{:T(128)} %bitcast.461, f32[]{:T(128)} %bitcast.462, f32[]{:T(128)} %bitcast.463, f32[]{:T(128)} %bitcast.464, f32[]{:T(128)} %bitcast.465, f32[]{:T(128)} %bitcast.466, f32[]{:T(128)} %bitcast.467, f32[]{:T(128)} %bitcast.468, f32[]{:T(128)} %bitcast.469, ...), kind=kLoop, calls=%fused_computation.100.clone.1 | loop fusion | flops 12451840 | bytes 526976 | tf_op jit(solution)/shard_map/while/body/eval_jaxpr/while/body/eval_jaxpr/jvp()/add | solution.py:39
  413.9 2.1 fusion.228
  417.2 1.9 bitcast_add_fusion.10
  419.1 2.0 rev.86
  423.7 2.5 select_reduce_fusion.33
  426.2 20.1 %fusion.230 = f32[32]{0:T(128)S(1)} fusion(f32[32]{0:T(128)S(1)} %get-tuple-element.2032, pred[]{:T(512)S(6)} %compare.44, f32[1]{0:T(128)} %bitcast.497, f32[1]{0:T(128)} %bitcast.498, f32[1]{0:T(128)} %bitcast.499, f32[1]{0:T(128)} %bitcast.500, f32[1]{0:T(128)} %bitcast.501, f32[1]{0:T(128)} %bitcast.502, f32[1]{0:T(128)} %bitcast.503, ...), kind=kLoop, calls=%fused_computation.175.clone.1 | loop fusion | flops 1056 | bytes 385 | tf_op jit(solution)/shard_map/while/body/eval_jaxpr/while/body/eval_jaxpr/add | solution.py:196
  447.6 2.5 constant_dynamic-slice_fusion.11
  451.1 2.1 tile.78
  453.1 1.7 slice.1302
  454.8 1.8 reshape.483
  456.6 1.7 slice.1303
  458.3 1.8 copy.169
  460.0 3.1 rev.85
  464.7 22.5 %add_add_fusion.7 = f32[128,512]{0,1:T(8,128)S(1)} fusion(f32[128,512]{0,1:T(8,128)} %rev.85, f32[]{:T(128)} %bitcast.461, f32[]{:T(128)} %bitcast.462, f32[]{:T(128)} %bitcast.463, f32[]{:T(128)} %bitcast.464, f32[]{:T(128)} %bitcast.465, f32[]{:T(128)} %bitcast.466, f32[]{:T(128)} %bitcast.467, f32[]{:T(128)} %bitcast.468, f32[]{:T(128)} %bitcast.469, ...), kind=kLoop, calls=%fused_computation.100.clone.1 | loop fusion | flops 12451840 | bytes 526976 | tf_op jit(solution)/shard_map/while/body/eval_jaxpr/while/body/eval_jaxpr/jvp()/add | solution.py:39
  489.1 2.1 fusion.228
  492.4 2.0 bitcast_add_fusion.10
  494.5 2.0 rev.86
  499.0 2.5 select_reduce_fusion.33
  501.6 20.1 %fusion.230 = f32[32]{0:T(128)S(1)} fusion(f32[32]{0:T(128)S(1)} %get-tuple-element.2032, pred[]{:T(512)S(6)} %compare.44, f32[1]{0:T(128)} %bitcast.497, f32[1]{0:T(128)} %bitcast.498, f32[1]{0:T(128)} %bitcast.499, f32[1]{0:T(128)} %bitcast.500, f32[1]{0:T(128)} %bitcast.501, f32[1]{0:T(128)} %bitcast.502, f32[1]{0:T(128)} %bitcast.503, ...), kind=kLoop, calls=%fused_computation.175.clone.1 | loop fusion | flops 1056 | bytes 385 | tf_op jit(solution)/shard_map/while/body/eval_jaxpr/while/body/eval_jaxpr/add | solution.py:196
  522.9 142.4 %all-reduce.34 = (f32[1024]{0:T(1024)}, f32[32]{0:T(128)}) all-reduce(f32[1024]{0:T(1024)S(1)} %get-tuple-element.956, f32[32]{0:T(128)S(1)} %get-tuple-element.957), channel_id=1, replica_groups=mesh['dp'=64,'ctx'=8] {'dp','ctx'}, use_global_device_ids=true, to_apply=%region_48.49 | all-reduce | flops 1056 | bytes 8448 | tf_op jit(solution)/shard_map/psum | solution.py:272
  665.3 3.0 fusion.136
  669.1 88.4 %while.80 = (s32[]{:T(128)}, f32[128,1024]{0,1:T(8,128)}, f32[128,1024]{0,1:T(8,128)}, s32[2]{0:T(128)S(1)}, bf16[1024,1024]{0,1:T(8,128)(2,1)}, /*index=5*/s32[...) while((s32[]{:T(128)}, f32[128,1024]{0,1:T(8,128)}, ...), condition=%wide.region_45.46_spmd.clone, body=%wide.region_44.45_spmd.clone.sunk | while | flops 560531328 | bytes 61329784 | solution.py:260
  670.3 1.5 constant_dynamic-slice_fusion.12
  674.1 1.9 fusion.237
  679.6 21.7 %add_add_fusion.8 = f32[512,128]{1,0:T(8,128)S(1)} fusion(f32[512,128]{1,0:T(8,128)S(1)} %rev.87, f32[]{:T(128)} %bitcast.540, f32[]{:T(128)} %bitcast.541, f32[]{:T(128)} %bitcast.542, f32[]{:T(128)} %bitcast.543, f32[]{:T(128)} %bitcast.544, f32[]{:T(128)} %bitcast.545, f32[]{:T(128)} %bitcast.546, f32[]{:T(128)} %bitcast.547, f32[]{:T(128)} %bitcast.548, ...), kind=kLoop, calls=%fused_computation.195.clone.1 | loop fusion | flops 12451840 | bytes 526976 | tf_op jit(solution)/shard_map/while/body/eval_jaxpr/while/body/eval_jaxpr/jvp()/add | solution.py:39
  701.7 3.8 fusion.241
  705.4 1.7 copy.176
  707.2 3.6 fusion.242
  710.8 2.3 bitcast_add_fusion.11
  714.3 1.5 constant_dynamic-slice_fusion.12
  718.1 1.9 fusion.237
  723.6 21.7 %add_add_fusion.8 = f32[512,128]{1,0:T(8,128)S(1)} fusion(f32[512,128]{1,0:T(8,128)S(1)} %rev.87, f32[]{:T(128)} %bitcast.540, f32[]{:T(128)} %bitcast.541, f32[]{:T(128)} %bitcast.542, f32[]{:T(128)} %bitcast.543, f32[]{:T(128)} %bitcast.544, f32[]{:T(128)} %bitcast.545, f32[]{:T(128)} %bitcast.546, f32[]{:T(128)} %bitcast.547, f32[]{:T(128)} %bitcast.548, ...), kind=kLoop, calls=%fused_computation.195.clone.1 | loop fusion | flops 12451840 | bytes 526976 | tf_op jit(solution)/shard_map/while/body/eval_jaxpr/while/body/eval_jaxpr/jvp()/add | solution.py:39
  745.7 3.8 fusion.241
  749.5 1.7 copy.176
  751.2 3.6 fusion.242
  754.8 2.6 bitcast_add_fusion.11
  758.7 7.9 reduce-scatter.2.cloned.1.call-done
  768.2 117.4 %all-reduce.37.cloned.1.call-done = f32[16,1024]{1,0:T(8,128)} async-done(((f32[16,1024]{1,0:T(8,128)}), f32[16,1024]{1,0:T(8,128)}) %all-reduce.37.cloned.1.call-update) | async-done | bytes 65552 | tf_op jit(solution)/shard_map/psum | solution.py:160
  885.6 1.5 copy.206
  (245 shorter events, 56.3 us)
Async XLA Ops:
  7.2 355.9 %copy-start = (bf16[1,128,1024]{2,1,0:T(8,128)(2,1)S(1)}, bf16[1,128,1024]{2,1,0:T(8,128)(2,1)}, u32[]{:S(2)}) copy-start(bf16[1,128,1024]{2,1,0:T(8,128)(2,1)} %param.20) | copy-start | bytes 786436
  7.2 96.8 %copy-start.6 = (bf16[1,128,1024]{2,1,0:T(8,128)(2,1)S(1)}, bf16[1,128,1024]{2,1,0:T(8,128)(2,1)}, u32[]{:S(2)}) copy-start(bf16[1,128,1024]{2,1,0:T(8,128)(2,1)} %param.16) | copy-start | bytes 786436
  7.2 6.5 copy-start.20
  7.2 6.9 copy-start.19
  7.2 96.8 %copy-start.18 = (f32[1024]{0:T(1024)S(1)}, f32[1024]{0:T(1024)}, u32[]{:S(2)}) copy-start(f32[1024]{0:T(1024)} %param.24) | copy-start | bytes 12292
  7.2 96.8 %copy-start.1 = (f32[32]{0:T(128)S(1)}, f32[32]{0:T(128)}, u32[]{:S(2)}) copy-start(f32[32]{0:T(128)} %param.25) | copy-start | bytes 388
  7.2 52.6 %all-gather.13.cloned.1.call-start = ((), (), s32[]{:S(2)}) async-start(), calls=%async_computation.5 | async-start | bytes 2359296 | tf_op jit(solution)/shard_map/all_gather | solution.py:109
  9.2 94.8 %all-gather.15.cloned.1.call-start = ((), (), s32[]{:S(2)}) async-start(), calls=%async_computation.6 | async-start | bytes 2359296 | tf_op jit(solution)/shard_map/all_gather | solution.py:108
  11.1 352.0 %all-gather.9.cloned.1.call-start = ((), (), s32[]{:S(2)}) async-start(), calls=%async_computation.1 | async-start | bytes 2129920 | tf_op jit(solution)/shard_map/all_gather | solution.py:147
  11.8 657.3 %all-gather.17.cloned.1.call-start = ((), (), s32[]{:S(2)}) async-start(), calls=%async_computation.7 | async-start | bytes 2359296 | tf_op jit(solution)/shard_map/all_gather | solution.py:221
  13.7 655.4 %all-gather.11.cloned.1.call-start = ((), (), s32[]{:S(2)}) async-start(), calls=%async_computation.2 | async-start | bytes 2359296 | tf_op jit(solution)/shard_map/all_gather | solution.py:222
  135.3 3.1 copy-start.9
  139.6 0.8 copy-start.10
  171.8 3.1 copy-start.9
  176.0 0.8 copy-start.10
  178.0 188.7 %copy-start.13 = (bf16[128,1024]{1,0:T(8,128)(2,1)}, bf16[128,1024]{1,0:T(8,128)(2,1)S(1)}, u32[]{:S(2)}) copy-start(bf16[128,1024]{1,0:T(8,128)(2,1)S(1)} %copy.114) | copy-start | bytes 786436
  178.1 187.5 %copy-start.16 = (bf16[1,128,1024]{2,1,0:T(8,128)(2,1)S(1)}, bf16[1,128,1024]{2,1,0:T(8,128)(2,1)}, u32[]{:S(2)}) copy-start(bf16[1,128,1024]{2,1,0:T(8,128)(2,1)} %param.19) | copy-start | bytes 786436
  366.7 399.9 %reduce-scatter.2.cloned.1.call-start = ((), (), s32[]{:S(2)}) async-start(), calls=%async_computation.3 | async-start | bytes 4259840 | tf_op jit(solution)/shard_map/reduce_scatter | solution.py:152
  369.6 1.6 copy-start.4
  369.6 516.0 %all-reduce.37.cloned.1.call-start = ((), (), s32[]{:S(2)}) async-start(), calls=%async_computation.4 | async-start | bytes 131072 | tf_op jit(solution)/shard_map/psum | solution.py:160
  411.9 2.0 copy-start.7
  411.9 2.0 copy-start.17
  419.1 4.6 copy-start.8
  487.1 2.0 copy-start.7
  487.1 2.0 copy-start.17
  494.5 4.6 copy-start.8
  670.3 2.8 copy-start.12
  673.1 0.9 copy-start.14
  673.2 3.0 copy-start.2
  701.3 4.1 copy-start.15
  701.6 5.5 copy-start.3
  701.6 5.5 copy-start.5
  714.3 2.8 copy-start.12
  717.1 1.0 copy-start.14
  717.2 3.0 copy-start.2
  745.3 4.1 copy-start.15
  745.7 5.5 copy-start.3
  745.7 5.5 copy-start.5
  757.4 9.9 %copy-start.11 = (f32[128,1024]{0,1:T(8,128)S(1)}, f32[128,1024]{0,1:T(8,128)}, u32[]{:S(2)}) copy-start(f32[128,1024]{0,1:T(8,128)} %get-tuple-element.955) | copy-start | bytes 1572868
Sparse Core Ops, SparseCore 0:
  10.8 49.0 all-gather.12
  62.5 41.4 all-gather.14
  106.1 256.8 all-gather.8
  365.0 83.8 all-gather.16
  451.4 37.4 all-gather.10
  491.6 274.9 reduce-scatter.1
  769.7 115.8 all-reduce.36
where the time goes:
time: 899 us; the launch traced here: 894 us
  waiting for transfers between devices  401 us (45%)
  other arithmetic  193 us (21%)
  blocking collectives  142 us (16%)
  local copies, waits for them, and re-layouts  97.3 us (11%)
  matrix products  40.8 us (5%)
  between operations  14.3 us (2%)
    all_gather x1, waiting for transfers between devices, on_device(): whole_rows = lax.all_gather(out_weight, 'dp', axis=0, tiled=True)  185 us
    psum x1, blocking collectives, on_device(): pos_grad, time_grad = lax.psum((pos_local, time_local), ('dp', 'ctx'))  142 us
    add x6, other arithmetic, block_bias(): return toeplitz(pos_table, offset, row_total, col_total) + timed  132 us
    psum x1, waiting for transfers between devices, on_device(): weight_grad = lax.psum(weight_part, 'ctx')  117 us
    all_gather x1, waiting for transfers between devices, on_device(): lax.all_gather(value_mine, 'ctx', axis=0, tiled=True)  45.8 us
    all_gather x1, waiting for transfers between devices, on_device(): lax.all_gather(key_mine, 'ctx', axis=0, tiled=True)  44.1 us
    add x2, other arithmetic, query_per_key(): carried[2] + time_part  40.2 us
  transfers between devices with their start and end apart: 7, of which 5 were waited for; matrix products, arithmetic and copies ran while one was open for 36% of the time, Pallas kernels for 0%

commit v1 on v0

v1 whole, which is shorter than its diff:
```python
import functools

import jax
import jax.numpy as jnp
from jax import lax
from jax.experimental import pallas as pl
from jax.experimental.pallas import tpu as pltpu
from jax.sharding import PartitionSpec as P

HEAD = 128
ROWS = 128
CTX = 8
COLS = 1024
PAD = 512
SLAB = PAD + ROWS
NX, NYL, NZ, NYH = 4, 2, 8, 4
WROWS = 16
EPSILON = 1e-06
FACTOR = HEAD ** (-0.5)
MASKED = -1e30
BUCKETS = 24
F32 = jnp.float32
BF16 = jnp.bfloat16
NT = (((1,), (1,)), ((), ()))


def dot(a, b):
    return jnp.dot(a, b, preferred_element_type=F32)


def dot_nt(a, b):
    return lax.dot_general(a, b, NT, preferred_element_type=F32)


def aligned(start, size=128):
    return pl.multiple_of(start, size)


def lanes_reversed(block):
    lane = lax.broadcasted_iota(jnp.int32, block.shape, 1)
    return jnp.take_along_axis(block, 127 - lane, axis=1, mode="promise_in_bounds")


def gate_of(scores):
    return 0.5 * jnp.tanh(0.5 * scores) + 0.5


def kernel(
    q_in, k_in, v_in, g_in, og_in, w_in, len_ref, stamp_ref, pos_ref, time_ref,
    lo_out, dq_out, dk_out, dv_out, gg_out, wg_out, pos_out, time_out,
    qh, kh, vh, doh, o_send, o_row, a_send, gate, ograd, mixed, mgrad, wbuf,
    stamp_pad, tz, bias, bucket, wts, wts_t, q_t, dk_t, dv_sum, d_send, pos_fold,
    lo_v, gg_v, w_send, w_own, w_r0, w_s0, w_r1, w_s1, w_r2, w_s2, w_r3, w_s3, w_land,
    b_v, b_r,
    loc, qkv_s, qkv_r, wz_s, wz_r, wx_s, wx_r, wy_s, wy_r, wc_s, wc_r,
    o_s, o_r, a_s, a_r, d_s, d_r, rc_s, rc_r, rx_s, rx_r, rz_s, rz_r, ry_s, ry_r,
    ag_s, ag_r, b_s, b_rs,
):
    dp = lax.axis_index("dp")
    me = lax.axis_index("ctx")
    z = lax.rem(dp, NZ)
    yl = lax.rem(lax.div(dp, NZ), NYL)
    x = lax.div(dp, NZ * NYL)
    core = lax.rem(me, 2)
    yh = lax.div(me, 2)

    def dp_of(xx, yy, zz):
        return (xx * NYL + yy) * NZ + zz

    def ctx_peer(k):
        return (dp, lax.rem(me + k, CTX))

    def z_peer(k):
        return (dp_of(x, yl, lax.rem(z + k, NZ)), me)

    def x_peer(k):
        return (dp_of(lax.rem(x + k, NX), yl, z), me)

    def xy_peer(k):
        return (dp_of(lax.rem(x + k // 2, NX), lax.rem(yl + k % 2, NYL), z), me)

    def y_peer(k):
        return (dp_of(x, lax.rem(yl + k // NYH, NYL), z), lax.rem(yh + k % NYH, NYH) * 2 + core)

    def remote(src, dst, send_sem, recv_sem, where):
        return pltpu.make_async_remote_copy(
            src_ref=src,
            dst_ref=dst,
            send_sem=send_sem,
            recv_sem=recv_sem,
            device_id=where,
            device_id_type=pl.DeviceIdType.MESH,
        )

    partners = [ctx_peer(k) for k in range(1, CTX)]
    partners += [z_peer(k) for k in range(1, NZ)]
    partners += [xy_peer(k) for k in range(1, NX * NYL)]
    partners += [y_peer(NYH + k) for k in range(1, NYH)]
    barrier = pltpu.get_barrier_semaphore()
    for where in partners:
        pl.semaphore_signal(barrier, inc=1, device_id=where, device_id_type=pl.DeviceIdType.MESH)

    my_rows = pl.ds(aligned(me * ROWS), ROWS)
    my_pad_rows = pl.ds(aligned(PAD + me * ROWS), ROWS)
    my_cols = pl.ds(aligned(me * HEAD), HEAD)
    half = pl.ds(aligned(core * 512), 512)
    w_rows = pl.ds(aligned(z * WROWS, WROWS), WROWS)
    own_copies = [
        pltpu.make_async_copy(q_in.at[0, :, my_cols], qh.at[my_rows], loc.at[0]),
        pltpu.make_async_copy(k_in.at[0, :, my_cols], kh.at[my_pad_rows], loc.at[1]),
        pltpu.make_async_copy(v_in.at[0, :, my_cols], vh.at[my_pad_rows], loc.at[2]),
        pltpu.make_async_copy(g_in.at[0], gate, loc.at[3]),
        pltpu.make_async_copy(og_in.at[0], ograd, loc.at[4]),
        pltpu.make_async_copy(w_in.at[:, half], wbuf.at[x, yl, w_rows, half], loc.at[5]),
    ]
    for copy in own_copies:
        copy.start()

    kh[0:PAD, :] = jnp.zeros((PAD, HEAD), BF16)
    vh[0:PAD, :] = jnp.zeros((PAD, HEAD), BF16)
    stamp_pad[:, 0:PAD] = jnp.zeros((1, PAD), jnp.int32)
    stamp_pad[:, PAD:] = stamp_ref[...]

    reversed_pos = lanes_reversed(pos_ref[...])
    line = jnp.concatenate(
        [reversed_pos[4 - b : 5 - b, :] for b in range(5)] + [jnp.zeros((1, 128), F32)], axis=1
    )
    sheet = pltpu.roll(jnp.broadcast_to(line, (ROWS, 768)), 1, 1)
    row_no = lax.broadcasted_iota(jnp.int32, (ROWS, 768), 0)
    for bit in range(7):
        rolled = pltpu.roll(sheet, 1 << bit, 1)
        sheet = jnp.where((row_no & (1 << bit)) != 0, rolled, sheet)
    tz[...] = sheet[:, 128:]

    pl.semaphore_wait(barrier, len(partners))

    def qkv_copy(a, k):
        where = ctx_peer(k)
        cols = pl.ds(aligned(where[1] * HEAD), HEAD)
        src = (q_in, k_in, v_in)[a].at[0, :, cols]
        dst = (qh.at[my_rows], kh.at[my_pad_rows], vh.at[my_pad_rows])[a]
        return remote(src, dst, qkv_s.at[a, k], qkv_r.at[a, k], where)

    def wz_copy(k):
        return remote(w_in.at[:, half], wbuf.at[x, yl, w_rows, half], wz_s.at[k], wz_r.at[k], z_peer(k))

    for k in range(1, NZ):
        wz_copy(k).start()
    for a in (0, 1, 2):
        for k in (3, 4, 5, 2, 6, 1, 7):
            qkv_copy(a, k).start()

    r_iota = lax.broadcasted_iota(jnp.int32, (ROWS, 128), 0)
    c_iota = lax.broadcasted_iota(jnp.int32, (ROWS, 128), 1)
    table = jnp.zeros((ROWS, 128), F32)
    for b in range(32):
        table = jnp.where(c_iota == b, time_ref[b], table)
    starts = []
    total = jnp.int32(0)
    for u in range(8):
        starts.append(total)
        total = total + len_ref[0, u]

    def bias_slab(i, unused):
        row_stamps = stamp_pad[:, pl.ds(aligned(PAD + i * ROWS), ROWS)]
        stamp_col = jnp.transpose(jnp.broadcast_to(row_stamps, (ROWS, 128)))
        place = r_iota + i * ROWS
        start = jnp.zeros((ROWS, 128), jnp.int32)
        for u in range(1, 8):
            start = jnp.where(place >= starts[u], jnp.maximum(start, starts[u]), start)
        first_col = start - (i * ROWS - PAD)
        for b in range(5):
            key_stamps = stamp_pad[:, pl.ds(aligned(i * ROWS + b * 128), 128)]
            gap = stamp_col - key_stamps
            number = 32 - lax.clz(gap)
            timed = jnp.take_along_axis(table, number, axis=1, mode="promise_in_bounds")
            col = c_iota + b * 128
            mask = (col >= first_col) & (col <= r_iota + PAD)
            cols = slice(b * 128, b * 128 + 128)
            bias[i, :, cols] = jnp.where(mask, tz[:, cols] + timed, MASKED)
            bucket[i, :, cols] = number
        return unused

    lax.fori_loop(0, CTX, bias_slab, 0)

    def wx_copy(k):
        mine = wbuf.at[x, yl, :, half]
        return remote(mine, mine, wx_s.at[k], wx_r.at[k], x_peer(k))

    own_copies[5].wait()
    for k in range(1, NZ):
        wz_copy(k).wait_recv()
    for k in range(1, NX):
        wx_copy(k).start()

    for copy in own_copies[:5]:
        copy.wait()
    for a in (0, 1, 2):
        for k in range(1, CTX):
            qkv_copy(a, k).wait_recv()

    def forward(i):
        rows = pl.ds(aligned(i * ROWS), ROWS)
        slab = pl.ds(aligned(i * ROWS), SLAB)
        pair_bias = bias[i]
        scores = dot_nt(qh[rows, :], kh[slab, :]) * FACTOR + pair_bias
        weights = jnp.where(pair_bias > 0.1 * MASKED, scores * gate_of(scores), 0.0).astype(BF16)
        bias[i] = scores
        wts[i] = weights
        return dot(weights, vh[slab, :]).astype(BF16)

    def o_copy(k):
        where = ctx_peer(k)
        return remote(o_send.at[where[1]], o_row.at[:, my_cols], o_s.at[k], o_r.at[k], where)

    def forward_step(k, unused):
        i = lax.rem(me + k, CTX)
        o_send[i] = forward(i)
        o_copy(k).start()
        return unused

    lax.fori_loop(1, CTX, forward_step, 0)
    o_row[:, my_cols] = forward(me)

    def wy_copy(way):
        peer_yh = lax.rem(yh + yl + (0 if way == 0 else NYH - 1), NYH)
        part = wbuf.at[pl.ds(2 * way, 2), yl, :, half]
        where = (dp_of(x, 1 - yl, z), peer_yh * 2 + core)
        return remote(part, part, wy_s.at[way], wy_r.at[way], where)

    def wc_copy():
        part = wbuf.at[:, :, :, half]
        return remote(part, part, wc_s.at[0], wc_r.at[0], (dp, yh * 2 + 1 - core))

    for k in range(1, NX):
        wx_copy(k).wait_recv()
    for way in range(2):
        wy_copy(way).start()

    def prepare(i, unused):
        scores = bias[i]
        sig = gate_of(scores)
        slope = sig * (1.0 + scores * (1.0 - sig))
        bias[i] = jnp.where(scores > 0.1 * MASKED, slope, 0.0)
        rows = pl.ds(aligned(i * ROWS), ROWS)
        q_t[:, rows] = jnp.transpose(qh[rows, :])
        wts_t[i] = jnp.transpose(wts[i])
        return unused

    lax.fori_loop(0, CTX, prepare, 0)
    dk_t[...] = jnp.zeros(dk_t.shape, F32)
    dv_sum[...] = jnp.zeros(dv_sum.shape, F32)

    for way in range(2):
        wy_copy(way).wait_recv()
    wc_copy().start()
    wc_copy().wait_recv()

    def mixed_grad_part(n, unused):
        block = wbuf[n].reshape(256, COLS)
        mgrad[:, pl.ds(aligned(n * 256), 256)] = dot_nt(ograd[...], block)
        return unused

    lax.fori_loop(0, NX, mixed_grad_part, 0)

    for k in range(1, CTX):
        o_copy(k).wait_recv()

    def rows_part(n, unused):
        rows = pl.ds(aligned(n * 32, 32), 32)
        attended = o_row[rows, :].astype(F32)
        center = attended - jnp.mean(attended, axis=1, keepdims=True)
        inv_dev = lax.rsqrt(jnp.mean(center * center, axis=1, keepdims=True) + EPSILON)
        normed = center * inv_dev
        gate_wide = gate[rows, :].astype(F32)
        grad = mgrad[rows, :]
        mixed[rows, :] = (normed * gate_wide).astype(BF16)
        gg_v[rows, :] = (grad * normed).astype(BF16)
        normed_grad = grad * gate_wide
        first = jnp.mean(normed_grad, axis=1, keepdims=True)
        second = jnp.mean(normed_grad * normed, axis=1, keepdims=True)
        a_send[rows, :] = (inv_dev * (normed_grad - first - normed * second)).astype(BF16)
        return unused

    lax.fori_loop(0, 4, rows_part, 0)

    def a_copy(k):
        where = ctx_peer(k)
        cols = pl.ds(aligned(where[1] * HEAD), HEAD)
        return remote(a_send.at[:, cols], doh.at[my_rows], a_s.at[k], a_r.at[k], where)

    for k in range(1, CTX):
        a_copy(k).start()
    doh[my_rows, :] = a_send[:, my_cols]

    other_half = pl.ds(aligned((1 - core) * 512), 512)

    def rc_copy(k):
        part = lax.rem(x + k, NX)
        return remote(w_send.at[part], w_r0.at[part], rc_s.at[k], rc_r.at[k], (dp, yh * 2 + 1 - core))

    def weight_part(k, unused):
        part = lax.rem(x + k, NX)
        turned = jnp.transpose(mixed[:, pl.ds(aligned(part * 256), 256)])
        w_send[part] = dot(turned, ograd[:, other_half]).astype(BF16)
        rc_copy(k).start()
        w_own[part] = dot(turned, ograd[:, half])
        return unused

    lax.fori_loop(1, NX + 1, weight_part, 0)

    def layer_part(n, unused):
        cols = pl.ds(aligned(n * 256), 256)
        block = wbuf[:, :, :, cols].reshape(COLS, 256)
        lo_v[:, cols] = dot(mixed[...], block).astype(BF16)
        return unused

    lax.fori_loop(0, 4, layer_part, 0)
    out_copies = [
        pltpu.make_async_copy(lo_v, lo_out.at[0], loc.at[6]),
        pltpu.make_async_copy(gg_v, gg_out.at[0], loc.at[7]),
    ]
    for copy in out_copies:
        copy.start()

    def rx_copy(k):
        part = lax.rem(x + k, NX)
        return remote(w_s0.at[part], w_r1.at[k], rx_s.at[k], rx_r.at[k], x_peer(k))

    def core_sum(k, unused):
        part = lax.rem(x + k, NX)
        rc_copy(k).wait_recv()
        w_s0[part] = (w_own[part] + w_r0[part].astype(F32)).astype(BF16)
        rx_copy(k).start()
        return unused

    lax.fori_loop(1, NX, core_sum, 0)
    rc_copy(NX).wait_recv()

    for k in range(1, CTX):
        a_copy(k).wait_recv()

    def backward(i):
        rows = pl.ds(aligned(i * ROWS), ROWS)
        slab = pl.ds(aligned(i * ROWS), SLAB)
        grad = doh[rows, :]
        score_grad = dot_nt(grad, vh[slab, :]) * bias[i]
        bias[i] = score_grad
        narrow = score_grad.astype(BF16)
        dk_t[:, slab] += dot(q_t[:, rows], narrow)
        dv_sum[slab, :] += dot(wts_t[i], grad)
        return (dot(narrow, kh[slab, :]) * FACTOR).astype(BF16)

    outs = (dq_out, dk_out, dv_out)

    def d_copy(a, k):
        where = ctx_peer(k)
        return remote(d_send.at[a, where[1]], outs[a].at[0, :, my_cols], d_s.at[a, k], d_r.at[a, k], where)

    def backward_step(k, unused):
        i = lax.rem(me + k, CTX)
        d_send[0, i] = backward(i)
        d_copy(0, k).start()
        return unused

    lax.fori_loop(1, CTX, backward_step, 0)
    d_send[0, me] = backward(me)

    def key_value_block(i):
        rows = pl.ds(aligned(PAD + i * ROWS), ROWS)
        d_send[1, i] = (jnp.transpose(dk_t[:, rows]) * FACTOR).astype(BF16)
        d_send[2, i] = dv_sum[rows, :].astype(BF16)

    def key_value_step(k, unused):
        key_value_block(lax.rem(me + k, CTX))
        d_copy(1, k).start()
        d_copy(2, k).start()
        return unused

    lax.fori_loop(1, CTX, key_value_step, 0)
    key_value_block(me)
    d_own = [
        pltpu.make_async_copy(d_send.at[a, me], outs[a].at[0, :, my_cols], loc.at[8 + a])
        for a in range(3)
    ]
    for copy in d_own:
        copy.start()

    def rz_copy(k):
        rows = pl.ds(aligned(lax.rem(z + k, NZ) * WROWS, WROWS), WROWS)
        return remote(w_s1.at[:, rows], w_r2.at[k], rz_s.at[k], rz_r.at[k], z_peer(k))

    for k in range(1, NX):
        rx_copy(k).wait_recv()

    def x_sum(n, unused):
        rows = pl.ds(aligned(n * 32, 32), 32)
        total = w_own[x, rows, :] + w_r0[x, rows, :].astype(F32)
        for k in range(1, NX):
            total = total + w_r1[k, rows, :].astype(F32)
        w_s1[lax.div(n, 4), pl.ds(aligned(lax.rem(n, 4) * 32, 32), 32), :] = total.astype(BF16)
        return unused

    lax.fori_loop(0, 8, x_sum, 0)
    for k in range(1, NZ):
        rz_copy(k).start()

    pos_fold[:, 0:128] = jnp.zeros((ROWS, 128), F32)

    def slab_sum(n, unused):
        rows = pl.ds(aligned(n * 8, 8), 8)
        total = bias[0, rows, :]
        for i in range(1, CTX):
            total = total + bias[i, rows, :]
        pos_fold[rows, 128:] = total
        return unused

    lax.fori_loop(0, 16, slab_sum, 0)
    fold = pos_fold[...]
    for count in (64, 32, 16, 8):
        fold = fold[:count] + pltpu.roll(fold[count : 2 * count], 768 - count, 1)
    row_no = lax.broadcasted_iota(jnp.int32, (8, 768), 0)
    for count in (4, 2, 1):
        fold = jnp.where((row_no & count) != 0, pltpu.roll(fold, 768 - count, 1), fold)
    fold = pltpu.roll(fold, 767, 1)
    fold = jnp.broadcast_to(jnp.sum(fold, axis=0, keepdims=True), (8, 768))
    row8 = lax.broadcasted_iota(jnp.int32, (8, 128), 0)
    lane8 = lax.broadcasted_iota(jnp.int32, (8, 128), 1)
    sums = jnp.zeros((8, 128), F32)
    for b in range(4):
        block = lanes_reversed(fold[:, (4 - b) * 128 : (5 - b) * 128])
        sums = jnp.where(row8 == b, block, sums)

    def histogram(n, totals):
        i = lax.div(n, 16)
        rows = pl.ds(aligned(lax.rem(n, 16) * 8, 8), 8)
        grads = bias[i, rows, :]
        numbers = bucket[i, rows, :]
        out = []
        for b in range(BUCKETS):
            hit = jnp.where(numbers == b, grads, 0.0)
            part = totals[b]
            for at in range(5):
                part = part + hit[:, at * 128 : at * 128 + 128]
            out.append(part)
        return tuple(out)

    totals = lax.fori_loop(
        0, 128, histogram, tuple(jnp.zeros((8, 128), F32) for unused in range(BUCKETS))
    )
    timed = jnp.zeros((8, 128), F32)
    for b in range(BUCKETS):
        whole = jnp.sum(jnp.sum(totals[b], axis=0, keepdims=True), axis=1, keepdims=True)
        timed = jnp.where(lane8 == b, whole, timed)
    sums = jnp.where(row8 == 4, timed, sums)

    slots = (me, z, x * NYL + yl)
    b_peers = (ctx_peer, z_peer, xy_peer)

    def b_copy(level, k):
        return remote(b_v.at[level], b_r.at[level, slots[level]], b_s.at[level, k], b_rs.at[level, k], b_peers[level](k))

    def b_start(level, value):
        b_v[level] = value
        b_r[level, slots[level]] = value
        for k in range(1, 8):
            b_copy(level, k).start()

    def b_finish(level):
        for k in range(1, 8):
            b_copy(level, k).wait_recv()
        value = b_r[level, 0]
        for slot in range(1, 8):
            value = value + b_r[level, slot]
        return value

    b_start(0, sums)

    def ry_copy(k):
        to_yl = lax.rem(yl + k // NYH, NYL)
        cols = pl.ds(aligned(lax.rem(yh + k % NYH, NYH) * 128), 128)
        return remote(w_s2.at[to_yl, :, cols], w_r3.at[k], ry_s.at[k], ry_r.at[k], y_peer(k))

    for k in range(1, NZ):
        rz_copy(k).wait_recv()
    z_rows = pl.ds(aligned(z * WROWS, WROWS), WROWS)
    total = w_s1[:, z_rows, :].astype(F32)
    for k in range(1, NZ):
        total = total + w_r2[k].astype(F32)
    w_s2[...] = total
    for k in range(1, NYL * NYH):
        ry_copy(k).start()

    b_start(1, b_finish(0))

    for k in range(1, NYL * NYH):
        ry_copy(k).wait_recv()
    piece = w_s2[yl, :, pl.ds(aligned(yh * 128), 128)]
    for k in range(1, NYL * NYH):
        piece = piece + w_r3[k]
    w_s3[...] = piece
    piece_cols = pl.ds(aligned(core * 512 + yh * 128), 128)
    w_land[:, piece_cols] = piece

    def ag_copy(k):
        return remote(w_s3, w_land.at[:, piece_cols], ag_s.at[k], ag_r.at[k], ctx_peer(k))

    for k in range(1, CTX):
        ag_copy(k).start()

    b_start(2, b_finish(1))

    for k in range(1, CTX):
        ag_copy(k).wait_recv()
    wg_out[...] = w_land[...]

    sums = b_finish(2)
    pos_out[...] = jnp.where(row8 < 4, sums, 0.0)
    time_out[...] = jnp.broadcast_to(sums[4:5, :], (8, 128))

    for a in (0, 1, 2):
        for k in range(1, CTX):
            d_copy(a, k).wait_recv()
    for copy in d_own + out_copies:
        copy.wait()
    for k in range(1, CTX):
        for a in range(3):
            qkv_copy(a, k).wait_send()
            d_copy(a, k).wait_send()
            b_copy(a, k).wait_send()
        wz_copy(k).wait_send()
        o_copy(k).wait_send()
        a_copy(k).wait_send()
        rz_copy(k).wait_send()
        ry_copy(k).wait_send()
        ag_copy(k).wait_send()
    for k in range(1, NX):
        wx_copy(k).wait_send()
        rx_copy(k).wait_send()
    for k in range(1, NX + 1):
        rc_copy(k).wait_send()
    for way in range(2):
        wy_copy(way).wait_send()
    wc_copy().wait_send()


def on_device(
    query_in, key_in, value_in, gate_in, out_grad, out_weight, lengths, stamps, pos_bias, time_bias
):
    dma = lambda *shape: pltpu.SemaphoreType.DMA(shape)
    vmem = pltpu.VMEM
    anywhere = pl.BlockSpec(memory_space=pl.ANY)
    in_vmem = pl.BlockSpec(memory_space=pltpu.VMEM)
    in_smem = pl.BlockSpec(memory_space=pltpu.SMEM)
    rows_shape = jax.ShapeDtypeStruct((1, ROWS, COLS), BF16)
    outs = pl.pallas_call(
        kernel,
        out_shape=[rows_shape] * 5
        + [
            jax.ShapeDtypeStruct((WROWS, COLS), F32),
            jax.ShapeDtypeStruct((8, 128), F32),
            jax.ShapeDtypeStruct((8, 128), F32),
        ],
        in_specs=[anywhere] * 6 + [in_smem, in_vmem, in_vmem, in_smem],
        out_specs=[anywhere] * 5 + [in_vmem] * 3,
        scratch_shapes=[
            vmem((COLS, HEAD), BF16),
            vmem((PAD + COLS, HEAD), BF16),
            vmem((PAD + COLS, HEAD), BF16),
            vmem((COLS, HEAD), BF16),
            vmem((CTX, ROWS, HEAD), BF16),
            vmem((ROWS, COLS), BF16),
            vmem((ROWS, COLS), BF16),
            vmem((ROWS, COLS), BF16),
            vmem((ROWS, COLS), BF16),
            vmem((ROWS, COLS), BF16),
            vmem((ROWS, COLS), F32),
            vmem((NX, NYL, NZ * WROWS, COLS), BF16),
            vmem((1, PAD + COLS), jnp.int32),
            vmem((ROWS, SLAB), F32),
            vmem((CTX, ROWS, SLAB), F32),
            vmem((CTX, ROWS, SLAB), jnp.int32),
            vmem((CTX, ROWS, SLAB), BF16),
            vmem((CTX, SLAB, ROWS), BF16),
            vmem((HEAD, COLS), BF16),
            vmem((HEAD, PAD + COLS), F32),
            vmem((PAD + COLS, HEAD), F32),
            vmem((3, CTX, ROWS, HEAD), BF16),
            vmem((ROWS, 768), F32),
            vmem((ROWS, COLS), BF16),
            vmem((ROWS, COLS), BF16),
            vmem((NX, 256, 512), BF16),
            vmem((NX, 256, 512), F32),
            vmem((NX, 256, 512), BF16),
            vmem((NX, 256, 512), BF16),
            vmem((NX, 256, 512), BF16),
            vmem((NYL, 128, 512), BF16),
            vmem((NZ, NYL, WROWS, 512), BF16),
            vmem((NYL, WROWS, 512), F32),
            vmem((NYL * NYH, WROWS, 128), F32),
            vmem((WROWS, 128), F32),
            vmem((WROWS, COLS), F32),
            vmem((3, 8, 128), F32),
            vmem((3, 8, 8, 128), F32),
            dma(12),
            dma(3, 8), dma(3, 8),
            dma(8), dma(8),
            dma(4), dma(4),
            dma(2), dma(2),
            dma(1), dma(1),
            dma(8), dma(8),
            dma(8), dma(8),
            dma(3, 8), dma(3, 8),
            dma(5), dma(5),
            dma(4), dma(4),
            dma(8), dma(8),
            dma(8), dma(8),
            dma(8), dma(8),
            dma(3, 8), dma(3, 8),
        ],
        compiler_params=pltpu.CompilerParams(
            collective_id=0, has_side_effects=True, vmem_limit_bytes=56 * 1024 * 1024
        ),
    )(
        query_in,
        key_in,
        value_in,
        gate_in,
        out_grad,
        out_weight,
        lengths,
        stamps,
        pos_bias.reshape(8, 128),
        time_bias,
    )
    layer_out, query_grad, key_grad, value_grad, gate_grad, weight_grad, pos, timed = outs
    return (
        layer_out,
        query_grad,
        key_grad,
        value_grad,
        gate_grad,
        weight_grad,
        pos.reshape(COLS),
        timed[0, :32],
    )


def solution(mesh):
    rows = P("dp", "ctx", None)
    owned = P("dp", None)
    return jax.shard_map(
        on_device,
        mesh=mesh,
        in_specs=(rows, rows, rows, rows, rows, owned, owned, owned, P(), P()),
        out_specs=(rows, rows, rows, rows, rows, owned, P(), P()),
        check_vma=False,
    )
```

time: 899 us -> 107 us (0.12)
  waiting for transfers between devices: 401 us -> 0 us
  other arithmetic: 193 us -> 0 us
  blocking collectives: 142 us -> 0 us
  Pallas kernels: 0 us -> 96.8 us
  local copies, waits for them, and re-layouts: 97.3 us -> 8.16 us
  matrix products: 40.8 us -> 0 us
  between operations: 14.3 us -> 0.65 us
    all_gather x5 -> x0, waiting for transfers between devices: 275 us -> none  [the longest x1 185 us: on_device(): whole_rows = lax.all_gather(out_weight, 'dp', axis=0, tiled=True)]
    add x28 -> x0, other arithmetic: 183 us -> none  [the longest x6 132 us: block_bias(): return toeplitz(pos_table, offset, row_total, col_total) + timed]
    psum x1 -> x0, blocking collectives: 142 us -> none  [on_device(): pos_grad, time_grad = lax.psum((pos_local, time_local), ('dp', 'ctx'))]
    psum x1 -> x0, waiting for transfers between devices: 117 us -> none  [on_device(): weight_grad = lax.psum(weight_part, 'ctx')]
    pallas_call x0 -> x1, Pallas kernels: none -> 96.8 us  [on_device(): pl.pallas_call(kernel, out_shape=[rows_shape] * 5 + [jax.ShapeDtypeStruct...]
    dot_general x17 -> x0, matrix products: 40.8 us -> none  [the longest x2 7.58 us: per_per_query(): jnp.einsum('hrc,rhd->chd', weights, split_heads(grad_block), preferred_el...]
    while x74 -> x0, local copies, waits for them, and re-layouts: 21.5 us -> none
    dynamic_slice x30 -> x0, local copies, waits for them, and re-layouts: 18.6 us -> none  [the longest x4 5.59 us: per_per_query(): lax.dynamic_slice_in_dim(grad_all, query_step * key_query_size, key_query...]
  transfers between devices with their start and end apart: 7 -> 0, of which waited for: 5 -> 0; matrix products, arithmetic and copies ran while one was open for 36% -> 0% of each run, Pallas kernels for 0% -> 0%
where the time goes in v1:
time: 107 us; the launch traced here: 106 us
  Pallas kernels  96.8 us (90%)
  local copies, waits for them, and re-layouts  8.16 us (8%)
    pallas_call x1, Pallas kernels, on_device(): pl.pallas_call(kernel, out_shape=[rows_shape] * 5 + [jax.ShapeDtypeStruct...  96.8 us
    unnamed x19, local copies, waits for them, and re-layouts  6.97 us

profile of v1, /device:TPU:1, one launch (start us, length us, event | category | flops | bytes accessed | tf_op | source)
XLA Modules:
  0.0 105.7 jit_solution(1922356106119023132)
XLA Ops:
  0.6 96.8 %shard_map.161 = (bf16[1,128,1024]{2,1,0:T(8,128)(2,1)}, bf16[1,128,1024]{2,1,0:T(8,128)(2,1)}, bf16[1,128,1024]{2,1,0:T(8,128)(2,1)}, bf16[1,128,1024]{2,1,0:T(...) custom-call(bf16[1,128,1024]{2,1,0:T(8,128)(2,1)} %q_in.1, ...), custom_call_target="tpu_custom_call" | custom-call | tf_op jit(solution)/shard_map/pallas_call | solution.py:556
  97.5 1.2 %slice_bitcast_fusion = f32[32]{0:T(128)} fusion(f32[8,128]{1,0:T(8,128)} %get-tuple-element.23), kind=kLoop, calls=%fused_computation | loop fusion | bytes 256 | tf_op jit(solution)/shard_map/squeeze | solution.py:645
  98.7 0.0 copy-start.3
  98.7 1.7 %copy.25 = bf16[1,128,1024]{2,1,0:T(8,128)(2,1)} copy(bf16[1,128,1024]{2,1,0:T(8,128)(2,1)} %get-tuple-element.32) | data formatting | bytes 524288
  100.4 0.0 copy-done.3
  100.4 0.0 copy-start.2
  100.4 0.7 copy.26
  101.1 0.3 copy-done.2
  101.4 0.0 copy-start.1
  101.4 0.7 copy.27
  102.1 0.3 copy-done.1
  102.5 0.0 copy-start
  102.5 0.7 copy.28
  103.2 0.3 copy-done
  103.5 0.0 copy-start.4
  103.5 0.7 copy.29
  104.2 0.2 copy-done.4
  104.4 0.0 copy-start.5
  104.4 0.6 copy.30
  105.0 0.0 copy-done.5
  105.1 0.6 copy.31
Async XLA Ops:
  98.7 1.7 %copy-start.3 = (bf16[1,128,1024]{2,1,0:T(8,128)(2,1)S(1)}, bf16[1,128,1024]{2,1,0:T(8,128)(2,1)}, u32[]{:S(2)}) copy-start(bf16[1,128,1024]{2,1,0:T(8,128)(2,1)} %get-tuple-element.33) | copy-start | bytes 786436
  100.4 1.0 copy-start.2
  101.4 1.0 copy-start.1
  102.5 1.0 copy-start
  103.5 0.9 copy-start.4
  104.4 0.7 copy-start.5

commit v2 on v1

v2 whole, which is shorter than its diff:
```python
import functools

import jax
import jax.numpy as jnp
from jax import lax
from jax.experimental import pallas as pl
from jax.experimental.pallas import tpu as pltpu
from jax.sharding import PartitionSpec as P

HEAD = 128
ROWS = 128
CTX = 8
COLS = 1024
PAD = 512
SLAB = PAD + ROWS
NX, NYL, NZ, NYH = 4, 2, 8, 4
WROWS = 16
EPSILON = 1e-06
FACTOR = HEAD ** (-0.5)
MASKED = -1e30
BUCKETS = 24
F32 = jnp.float32
BF16 = jnp.bfloat16
NT = (((1,), (1,)), ((), ()))


def dot(a, b):
    return jnp.dot(a, b, preferred_element_type=F32)


def dot_nt(a, b):
    return lax.dot_general(a, b, NT, preferred_element_type=F32)


def aligned(start, size=128):
    return pl.multiple_of(start, size)


def lanes_reversed(block):
    lane = lax.broadcasted_iota(jnp.int32, block.shape, 1)
    return jnp.take_along_axis(block, 127 - lane, axis=1, mode="promise_in_bounds")


def gate_of(scores):
    return 0.5 * jnp.tanh(0.5 * scores) + 0.5


def kernel(
    q_in, k_in, v_in, g_in, og_in, w_in, len_in, stamp_in, pos_in, time_in,
    lo_out, dq_out, dk_out, dv_out, gg_out, wg_out, pos_out, time_out,
    len_ref, stamp_ref, pos_ref, time_ref, table_v,
    qh, kh, vh, doh, o_send, o_row, a_send, gate, ograd, mixed, mgrad, wbuf,
    stamp_pad, tz, bias, bucket, wts, wts_t, q_t, dk_t, d_send, pos_fold,
    lo_v, gg_v, w_send, w_own, w_r0, w_s0, w_ax, w_a1, w_az, w_bz, w_b1, w_bx, w_s2, w_r3, w_s3, w_land,
    b_v, b_r,
    loc, qkv_s, qkv_r, wz_s, wz_r, wx_s, wx_r, wy_s, wy_r, wc_s, wc_r,
    o_s, o_r, a_s, a_r, d_s, d_r, rc_s, rc_r, rx_s, rx_r, rz_s, rz_r, ry_s, ry_r,
    ag_s, ag_r, b_s, b_rs,
):
    dp = lax.axis_index("dp")
    me = lax.axis_index("ctx")
    z = lax.rem(dp, NZ)
    yl = lax.rem(lax.div(dp, NZ), NYL)
    x = lax.div(dp, NZ * NYL)
    core = lax.rem(me, 2)
    yh = lax.div(me, 2)

    def dp_of(xx, yy, zz):
        return (xx * NYL + yy) * NZ + zz

    def ctx_peer(k):
        return (dp, lax.rem(me + k, CTX))

    def z_peer(k):
        return (dp_of(x, yl, lax.rem(z + k, NZ)), me)

    def x_peer(k):
        return (dp_of(lax.rem(x + k, NX), yl, z), me)

    def xy_peer(k):
        return (dp_of(lax.rem(x + k // 2, NX), lax.rem(yl + k % 2, NYL), z), me)

    def y_peer(k):
        return (dp_of(x, lax.rem(yl + k // NYH, NYL), z), lax.rem(yh + k % NYH, NYH) * 2 + core)

    def remote(src, dst, send_sem, recv_sem, where):
        return pltpu.make_async_remote_copy(
            src_ref=src,
            dst_ref=dst,
            send_sem=send_sem,
            recv_sem=recv_sem,
            device_id=where,
            device_id_type=pl.DeviceIdType.MESH,
        )

    partners = [ctx_peer(k) for k in range(1, CTX)]
    partners += [z_peer(k) for k in range(1, NZ)]
    partners += [xy_peer(k) for k in range(1, NX * NYL)]
    partners += [y_peer(NYH + k) for k in range(1, NYH)]
    barrier = pltpu.get_barrier_semaphore()
    for where in partners:
        pl.semaphore_signal(barrier, inc=1, device_id=where, device_id_type=pl.DeviceIdType.MESH)

    my_rows = pl.ds(aligned(me * ROWS), ROWS)
    my_pad_rows = pl.ds(aligned(PAD + me * ROWS), ROWS)
    my_cols = pl.ds(aligned(me * HEAD), HEAD)
    half = pl.ds(aligned(core * 512), 512)
    w_rows = pl.ds(aligned(z * WROWS, WROWS), WROWS)
    own_copies = [
        pltpu.make_async_copy(q_in.at[0, :, my_cols], qh.at[my_rows], loc.at[0]),
        pltpu.make_async_copy(k_in.at[0, :, my_cols], kh.at[my_pad_rows], loc.at[1]),
        pltpu.make_async_copy(v_in.at[0, :, my_cols], vh.at[my_pad_rows], loc.at[2]),
        pltpu.make_async_copy(g_in.at[0], gate, loc.at[3]),
        pltpu.make_async_copy(og_in.at[0], ograd, loc.at[4]),
        pltpu.make_async_copy(w_in.at[:, half], wbuf.at[x, yl, w_rows, half], loc.at[5]),
    ]
    small_copies = [
        pltpu.make_async_copy(len_in, len_ref, loc.at[11]),
        pltpu.make_async_copy(stamp_in, stamp_ref, loc.at[12]),
        pltpu.make_async_copy(pos_in, pos_ref, loc.at[13]),
        pltpu.make_async_copy(time_in, time_ref, loc.at[14]),
    ]
    for copy in small_copies:
        copy.start()
    pl.semaphore_wait(barrier, len(partners))

    def qkv_copy(a, k):
        where = ctx_peer(k)
        cols = pl.ds(aligned(where[1] * HEAD), HEAD)
        src = (q_in, k_in, v_in)[a].at[0, :, cols]
        dst = (qh.at[my_rows], kh.at[my_pad_rows], vh.at[my_pad_rows])[a]
        return remote(src, dst, qkv_s.at[a, k], qkv_r.at[a, k], where)

    def wy_copy():
        return remote(w_in.at[:, half], wbuf.at[x, yl, w_rows, half], wy_s.at[0], wy_r.at[0], (dp_of(x, 1 - yl, z), me))

    def wz_copy(which, k):
        dst = wbuf.at[x, yl if which == 0 else 1 - yl, w_rows, half]
        src = w_in.at[:, half] if which == 0 else dst
        return remote(src, dst, wz_s.at[which, k], wz_r.at[which, k], z_peer(k))

    def wx_copy(which, k):
        part = wbuf.at[x, yl if which == 0 else 1 - yl, :, half]
        return remote(part, part, wx_s.at[which, k], wx_r.at[which, k], x_peer(k))

    def wc_copy(k):
        part = wbuf.at[lax.rem(x + NX - k, NX), :, :, half]
        return remote(part, part, wc_s.at[k], wc_r.at[k], (dp, yh * 2 + 1 - core))

    wy_copy().start()
    for k in range(1, NZ):
        wz_copy(0, k).start()
    for k in (3, 4, 5, 2, 6, 1, 7):
        qkv_copy(0, k).start()
        qkv_copy(1, k).start()
    for copy in own_copies:
        copy.start()
    for k in (3, 4, 5, 2, 6, 1, 7):
        qkv_copy(2, k).start()

    kh[0:PAD, :] = jnp.zeros((PAD, HEAD), BF16)
    vh[0:PAD, :] = jnp.zeros((PAD, HEAD), BF16)
    doh[COLS:, :] = jnp.zeros((PAD, HEAD), BF16)
    for j in range(4, CTX):
        for t in range(CTX - j, 5):
            wts_t[j + 4, :, t * 128 : t * 128 + 128] = jnp.zeros((128, 128), BF16)
    dk_t[...] = jnp.zeros(dk_t.shape, F32)
    stamp_pad[:, 0:PAD] = jnp.zeros((1, PAD), jnp.int32)
    for copy in small_copies:
        copy.wait()
    stamp_pad[:, PAD:] = stamp_ref[...]

    reversed_pos = lanes_reversed(pos_ref[...])
    line = jnp.concatenate(
        [reversed_pos[4 - b : 5 - b, :] for b in range(5)] + [jnp.zeros((1, 128), F32)], axis=1
    )
    sheet = pltpu.roll(jnp.broadcast_to(line, (ROWS, 768)), 1, 1)
    row_no = lax.broadcasted_iota(jnp.int32, (ROWS, 768), 0)
    for bit in range(7):
        rolled = pltpu.roll(sheet, 1 << bit, 1)
        sheet = jnp.where((row_no & (1 << bit)) != 0, rolled, sheet)
    tz[...] = sheet[:, 128:]

    r_iota = lax.broadcasted_iota(jnp.int32, (ROWS, 128), 0)
    c_iota = lax.broadcasted_iota(jnp.int32, (ROWS, 128), 1)
    table = jnp.zeros((ROWS, 128), F32)
    for b in range(32):
        table = jnp.where(c_iota == b, time_ref[b], table)
    starts = []
    total = jnp.int32(0)
    for u in range(8):
        starts.append(total)
        total = total + len_ref[0, u]

    def bias_slab(i, unused):
        row_stamps = stamp_pad[:, pl.ds(aligned(PAD + i * ROWS), ROWS)]
        stamp_col = jnp.transpose(jnp.broadcast_to(row_stamps, (ROWS, 128)))
        place = r_iota + i * ROWS
        start = jnp.zeros((ROWS, 128), jnp.int32)
        for u in range(1, 8):
            start = jnp.where(place >= starts[u], jnp.maximum(start, starts[u]), start)
        first_col = start - (i * ROWS - PAD)
        numbers = []
        for b in range(5):
            key_stamps = stamp_pad[:, pl.ds(aligned(i * ROWS + b * 128), 128)]
            number = 32 - lax.clz(stamp_col - key_stamps)
            timed = jnp.take_along_axis(table, number, axis=1, mode="promise_in_bounds")
            col = c_iota + b * 128
            mask = (col >= first_col) & (col <= r_iota + PAD)
            cols = slice(b * 128, b * 128 + 128)
            bias[i, :, cols] = jnp.where(mask, tz[:, cols] + timed, MASKED)

            numbers.append(number)
            if b in (1, 2, 3):
                bucket[i, :, cols] = number
        bucket[i, :, 512:] = jnp.where(c_iota <= r_iota, numbers[4], numbers[0])
        return unused

    lax.fori_loop(0, CTX, bias_slab, 0)

    wy_copy().wait_recv()
    for k in range(1, NZ):
        wz_copy(1, k).start()
    own_copies[5].wait()
    for k in range(1, NZ):
        wz_copy(0, k).wait_recv()
    for k in range(1, NX):
        wx_copy(0, k).start()
    for k in range(1, NZ):
        wz_copy(1, k).wait_recv()
    for k in range(1, NX):
        wx_copy(1, k).start()
    wc_copy(0).start()

    for copy in own_copies[:5]:
        copy.wait()
    for a in (0, 1):
        for k in range(1, CTX):
            qkv_copy(a, k).wait_recv()

    def weigh(i, unused):
        rows = pl.ds(aligned(i * ROWS), ROWS)
        slab = pl.ds(aligned(i * ROWS), SLAB)
        pair_bias = bias[i]
        mask = pair_bias > 0.1 * MASKED
        scores = dot_nt(qh[rows, :], kh[slab, :]) * FACTOR + pair_bias
        sig = gate_of(scores)
        weights = jnp.where(mask, scores * sig, 0.0).astype(BF16)
        wts[i] = weights
        bias[i] = jnp.where(mask, sig * (1.0 + scores * (1.0 - sig)), 0.0)
        for b in range(5):
            turned = jnp.transpose(weights[:, b * 128 : b * 128 + 128])
            wts_t[i + b, :, (4 - b) * 128 : (5 - b) * 128] = turned
        q_t[:, rows] = jnp.transpose(qh[rows, :])
        return unused

    lax.fori_loop(0, CTX, weigh, 0)

    def attend(i):
        slab = pl.ds(aligned(i * ROWS), SLAB)
        return dot(wts[i], vh[slab, :]).astype(BF16)

    def part_rows(part):
        return pl.ds(part * 64, 64)

    def o_copy(part, k):
        where = ctx_peer(k)
        rows = part_rows(part)
        return remote(
            o_send.at[where[1], rows], o_row.at[rows, my_cols], o_s.at[part, k], o_r.at[part, k], where
        )

    def attend_step(k, unused):
        i = lax.rem(me + k, CTX)
        o_send[i] = attend(i)
        o_copy(0, k).start()
        return unused

    for k in range(1, CTX):
        qkv_copy(2, k).wait_recv()
    lax.fori_loop(1, CTX, attend_step, 0)
    for k in range(1, CTX):
        o_copy(1, k).start()
    o_row[:, my_cols] = attend(me)

    for k in range(1, NX):
        for which in range(2):
            wx_copy(which, k).wait_recv()
        wc_copy(k).start()
    for k in range(NX):
        wc_copy(k).wait_recv()

    def mixed_grad_part(n, unused):
        block = wbuf[n].reshape(256, COLS)
        mgrad[:, pl.ds(aligned(n * 256), 256)] = dot_nt(ograd[...], block)
        return unused

    lax.fori_loop(0, NX, mixed_grad_part, 0)

    def rows_part(n, unused):
        rows = pl.ds(aligned(n * 32, 32), 32)
        attended = o_row[rows, :].astype(F32)
        center = attended - jnp.mean(attended, axis=1, keepdims=True)
        inv_dev = lax.rsqrt(jnp.mean(center * center, axis=1, keepdims=True) + EPSILON)
        normed = center * inv_dev
        gate_wide = gate[rows, :].astype(F32)
        grad = mgrad[rows, :]
        mixed[rows, :] = (normed * gate_wide).astype(BF16)
        gg_v[rows, :] = (grad * normed).astype(BF16)
        normed_grad = grad * gate_wide
        first = jnp.mean(normed_grad, axis=1, keepdims=True)
        second = jnp.mean(normed_grad * normed, axis=1, keepdims=True)
        a_send[rows, :] = (inv_dev * (normed_grad - first - normed * second)).astype(BF16)
        return unused

    def a_copy(part, k):
        where = ctx_peer(k)
        cols = pl.ds(aligned(where[1] * HEAD), HEAD)
        rows = pl.ds(aligned(me * ROWS + part * 64, 64), 64)
        return remote(
            a_send.at[part_rows(part), cols], doh.at[rows], a_s.at[part, k], a_r.at[part, k], where
        )

    for part in range(2):
        for k in range(1, CTX):
            o_copy(part, k).wait_recv()
        lax.fori_loop(2 * part, 2 * part + 2, rows_part, 0)
        for k in range(1, CTX):
            a_copy(part, k).start()
    doh[my_rows, :] = a_send[:, my_cols]

    other_half = pl.ds(aligned((1 - core) * 512), 512)

    def rc_copy(k):
        part = lax.rem(x + k, NX)
        return remote(w_send.at[part], w_r0.at[part], rc_s.at[k], rc_r.at[k], (dp, yh * 2 + 1 - core))

    def weight_part(k, unused):
        part = lax.rem(x + k, NX)
        turned = jnp.transpose(mixed[:, pl.ds(aligned(part * 256), 256)])
        w_send[part] = dot(turned, ograd[:, other_half]).astype(BF16).reshape(2, 128, 512)
        rc_copy(k).start()
        w_own[part] = dot(turned, ograd[:, half]).reshape(2, 128, 512)
        return unused

    lax.fori_loop(1, NX + 1, weight_part, 0)

    wide, narrow_cols = pl.ds(0, 384), pl.ds(384, 128)

    def z_rows(k):
        return pl.ds(aligned(lax.rem(z + k, NZ) * WROWS, WROWS), WROWS)

    def ax_copy(k):
        part = lax.rem(x + k, NX)
        return remote(w_s0.at[part, :, :, wide], w_ax.at[k], rx_s.at[0, k], rx_r.at[0, k], x_peer(k))

    def az_copy(k):
        return remote(w_a1.at[:, z_rows(k)], w_az.at[k], rz_s.at[0, k], rz_r.at[0, k], z_peer(k))

    def bz_copy(k):
        src = w_s0.at[:, :, z_rows(k), narrow_cols]
        return remote(src, w_bz.at[k], rz_s.at[1, k], rz_r.at[1, k], z_peer(k))

    def bx_copy(k):
        part = lax.rem(x + k, NX)
        return remote(w_b1.at[part], w_bx.at[k], rx_s.at[1, k], rx_r.at[1, k], x_peer(k))

    def core_sum(k):
        part = lax.rem(x + k, NX)
        rc_copy(k).wait_recv()
        w_s0[part] = (w_own[part] + w_r0[part].astype(F32)).astype(BF16)

    def core_step(k, unused):
        core_sum(k)
        ax_copy(k).start()
        return unused

    lax.fori_loop(1, NX, core_step, 0)
    core_sum(NX)
    for k in range(1, NZ):
        bz_copy(k).start()

    def layer_part(n, unused):
        cols = pl.ds(aligned(n * 256), 256)
        block = wbuf[:, :, :, cols].reshape(COLS, 256)
        lo_v[:, cols] = dot(mixed[...], block).astype(BF16)
        return unused

    lax.fori_loop(0, 4, layer_part, 0)
    out_copies = [
        pltpu.make_async_copy(lo_v, lo_out.at[0], loc.at[6]),
        pltpu.make_async_copy(gg_v, gg_out.at[0], loc.at[7]),
    ]
    for copy in out_copies:
        copy.start()


    for part in range(2):
        for k in range(1, CTX):
            a_copy(part, k).wait_recv()

    outs = (dq_out, dk_out, dv_out)

    def d_copy(a, k):
        where = ctx_peer(k)
        return remote(d_send.at[a, where[1]], outs[a].at[0, :, my_cols], d_s.at[a, k], d_r.at[a, k], where)

    def value_block(i):
        slab = pl.ds(aligned(i * ROWS), SLAB)
        d_send[2, i] = dot(wts_t[i + 4], doh[slab, :]).astype(BF16)

    def value_step(k, unused):
        value_block(lax.rem(me + k, CTX))
        d_copy(2, k).start()
        return unused

    lax.fori_loop(1, CTX, value_step, 0)
    value_block(me)

    def query_block(i):
        rows = pl.ds(aligned(i * ROWS), ROWS)
        slab = pl.ds(aligned(i * ROWS), SLAB)
        score_grad = dot_nt(doh[rows, :], vh[slab, :]) * bias[i]
        bias[i] = score_grad
        narrow = score_grad.astype(BF16)
        dk_t[:, slab] += dot(q_t[:, rows], narrow)
        d_send[0, i] = (dot(narrow, kh[slab, :]) * FACTOR).astype(BF16)

    def query_step(k, unused):
        query_block(lax.rem(me + k, CTX))
        d_copy(0, k).start()
        return unused

    lax.fori_loop(1, CTX, query_step, 0)
    query_block(me)

    pos_fold[:, 0:128] = jnp.zeros((ROWS, 128), F32)

    def slab_sum(n, unused):
        rows = pl.ds(aligned(n * 8, 8), 8)
        total = bias[0, rows, :]
        for i in range(1, CTX):
            total = total + bias[i, rows, :]
        pos_fold[rows, 128:] = total
        return unused

    lax.fori_loop(0, 16, slab_sum, 0)
    fold = pos_fold[...]
    for count in (64, 32, 16, 8):
        fold = fold[:count] + pltpu.roll(fold[count : 2 * count], 768 - count, 1)
    row_no = lax.broadcasted_iota(jnp.int32, (8, 768), 0)
    for count in (4, 2, 1):
        fold = jnp.where((row_no & count) != 0, pltpu.roll(fold, 768 - count, 1), fold)
    fold = pltpu.roll(fold, 767, 1)
    fold = jnp.broadcast_to(jnp.sum(fold, axis=0, keepdims=True), (8, 768))
    row8 = lax.broadcasted_iota(jnp.int32, (8, 128), 0)
    sums = jnp.zeros((8, 128), F32)
    for b in range(4):
        block = lanes_reversed(fold[:, (4 - b) * 128 : (5 - b) * 128])
        sums = jnp.where(row8 == b, block, sums)

    def histogram(first, blocks):
        def step(n, totals):
            i = first + lax.div(n, 16)
            rows = pl.ds(aligned(lax.rem(n, 16) * 8, 8), 8)
            grads = [bias[i, rows, 0:128] + bias[i, rows, 512:640]]
            numbers = [bucket[i, rows, 512:640]]
            for b in blocks:
                grads.append(bias[i, rows, b * 128 : b * 128 + 128])
                numbers.append(bucket[i, rows, b * 128 : b * 128 + 128])
            out = []
            for number in range(BUCKETS):
                part = totals[number]
                for at in range(len(grads)):
                    part = part + jnp.where(numbers[at] == number, grads[at], 0.0)
                out.append(part)
            return tuple(out)

        return step

    totals = tuple(jnp.zeros((8, 128), F32) for unused in range(BUCKETS))
    for first, count, blocks in ((0, 1, ()), (1, 1, (3,)), (2, 1, (2, 3)), (3, 1, (1, 2, 3))):
        totals = lax.fori_loop(0, 16 * count, histogram(first, blocks), totals)
    for k in range(1, NX):
        ax_copy(k).wait_recv()

    def a_sum(n, unused):
        to_yl = lax.div(n, 4)
        rows = pl.ds(aligned(lax.rem(n, 4) * 32, 32), 32)
        total = w_own[x, to_yl, rows, wide] + w_r0[x, to_yl, rows, wide].astype(F32)
        for k in range(1, NX):
            total = total + w_ax[k, to_yl, rows, :].astype(F32)
        w_a1[to_yl, rows, :] = total.astype(BF16)
        return unused

    lax.fori_loop(0, 8, a_sum, 0)
    for k in range(1, NZ):
        az_copy(k).start()
    for k in range(1, NZ):
        bz_copy(k).wait_recv()

    def b_sum(n, unused):
        total = w_own[n, :, z_rows(0), narrow_cols] + w_r0[n, :, z_rows(0), narrow_cols].astype(F32)
        for k in range(1, NZ):
            total = total + w_bz[k, n].astype(F32)
        w_b1[n] = total.astype(BF16)
        return unused

    lax.fori_loop(0, NX, b_sum, 0)
    for k in range(1, NX):
        bx_copy(k).start()

    totals = lax.fori_loop(0, 16 * 4, histogram(4, (1, 2, 3)), totals)
    lane8 = lax.broadcasted_iota(jnp.int32, (8, 128), 1)
    timed = jnp.zeros((8, 128), F32)
    for b in range(BUCKETS):
        whole = jnp.sum(jnp.sum(totals[b], axis=0, keepdims=True), axis=1, keepdims=True)
        timed = jnp.where(lane8 == b, whole, timed)
    sums = jnp.where(row8 == 4, timed, sums)

    slots = (me, z, x * NYL + yl)
    b_peers = (ctx_peer, z_peer, xy_peer)

    def b_copy(level, k):
        return remote(b_v.at[level], b_r.at[level, slots[level]], b_s.at[level, k], b_rs.at[level, k], b_peers[level](k))

    def b_start(level, value):
        b_v[level] = value
        b_r[level, slots[level]] = value
        for k in range(1, 8):
            b_copy(level, k).start()

    def b_finish(level):
        for k in range(1, 8):
            b_copy(level, k).wait_recv()
        value = b_r[level, 0]
        for slot in range(1, 8):
            value = value + b_r[level, slot]
        return value

    b_start(0, sums)

    def key_block(i):
        rows = pl.ds(aligned(PAD + i * ROWS), ROWS)
        d_send[1, i] = (jnp.transpose(dk_t[:, rows]) * FACTOR).astype(BF16)

    def key_step(k, unused):
        key_block(lax.rem(me + k, CTX))
        d_copy(1, k).start()
        return unused

    lax.fori_loop(1, CTX, key_step, 0)
    key_block(me)
    d_own = [
        pltpu.make_async_copy(d_send.at[a, me], outs[a].at[0, :, my_cols], loc.at[8 + a])
        for a in range(3)
    ]
    for copy in d_own:
        copy.start()

    def ry_copy(k):
        to_yl = lax.rem(yl + k // NYH, NYL)
        cols = pl.ds(aligned(lax.rem(yh + k % NYH, NYH) * 128), 128)
        return remote(w_s2.at[to_yl, :, cols], w_r3.at[k], ry_s.at[k], ry_r.at[k], y_peer(k))

    for k in range(1, NZ):
        az_copy(k).wait_recv()
    total = w_a1[:, z_rows(0), :].astype(F32)
    for k in range(1, NZ):
        total = total + w_az[k].astype(F32)
    w_s2[:, :, wide] = total
    for k in range(1, NX):
        bx_copy(k).wait_recv()
    total = w_b1[x].astype(F32)
    for k in range(1, NX):
        total = total + w_bx[k].astype(F32)
    w_s2[:, :, narrow_cols] = total
    for k in range(1, NYL * NYH):
        ry_copy(k).start()

    b_start(1, b_finish(0))

    for k in range(1, NYL * NYH):
        ry_copy(k).wait_recv()
    piece = w_s2[yl, :, pl.ds(aligned(yh * 128), 128)]
    for k in range(1, NYL * NYH):
        piece = piece + w_r3[k]
    w_s3[...] = piece
    piece_cols = pl.ds(aligned(core * 512 + yh * 128), 128)
    w_land[:, piece_cols] = piece

    def ag_copy(k):
        return remote(w_s3, w_land.at[:, piece_cols], ag_s.at[k], ag_r.at[k], ctx_peer(k))

    for k in range(1, CTX):
        ag_copy(k).start()

    b_start(2, b_finish(1))

    for k in range(1, CTX):
        ag_copy(k).wait_recv()
    wg_copy = pltpu.make_async_copy(w_land, wg_out, loc.at[15])
    wg_copy.start()

    sums = b_finish(2)
    table_v[0] = jnp.where(row8 < 4, sums, 0.0)
    table_v[1] = jnp.broadcast_to(sums[4:5, :], (8, 128))
    table_copies = [
        pltpu.make_async_copy(table_v.at[0], pos_out, loc.at[16]),
        pltpu.make_async_copy(table_v.at[1], time_out, loc.at[17]),
    ]
    for copy in table_copies:
        copy.start()

    for k in range(1, CTX):
        for a in range(3):
            qkv_copy(a, k).wait_send()
            b_copy(a, k).wait_send()
        for part in range(2):
            wz_copy(part, k).wait_send()
            o_copy(part, k).wait_send()
            a_copy(part, k).wait_send()
        az_copy(k).wait_send()
        bz_copy(k).wait_send()
        ry_copy(k).wait_send()
        ag_copy(k).wait_send()
    for k in range(1, NX):
        for which in range(2):
            wx_copy(which, k).wait_send()
        ax_copy(k).wait_send()
        bx_copy(k).wait_send()
    for k in range(1, NX + 1):
        rc_copy(k).wait_send()
    for k in range(NX):
        wc_copy(k).wait_send()
    wy_copy().wait_send()
    for copy in d_own + out_copies + table_copies + [wg_copy]:
        copy.wait()
    for a in (2, 0, 1):
        for k in range(1, CTX):
            d_copy(a, k).wait_recv()
            d_copy(a, k).wait_send()


def hand_over(*refs):
    given, results, held, sems = refs[:7], refs[8:15], refs[16:23], refs[23]
    reads = [pltpu.make_async_copy(given[n], held[n], sems.at[0, n]) for n in range(7)]
    writes = [pltpu.make_async_copy(held[n], results[n], sems.at[1, n]) for n in range(7)]
    for copy in reads:
        copy.start()
    refs[15][...] = refs[7][0, 0:32]
    for read, write in zip(reads, writes):
        read.wait()
        write.start()
    for copy in writes:
        copy.wait()


def on_device(
    query_in, key_in, value_in, gate_in, out_grad, out_weight, lengths, stamps, pos_bias, time_bias
):
    dma = lambda *shape: pltpu.SemaphoreType.DMA(shape)
    vmem = pltpu.VMEM
    anywhere = pl.BlockSpec(memory_space=pl.ANY)
    in_vmem = pl.BlockSpec(memory_space=pltpu.VMEM)
    rows_shape = jax.ShapeDtypeStruct((1, ROWS, COLS), BF16)
    outs = pl.pallas_call(
        kernel,
        out_shape=[rows_shape] * 5
        + [
            jax.ShapeDtypeStruct((WROWS, COLS), F32),
            jax.ShapeDtypeStruct((8, 128), F32),
            jax.ShapeDtypeStruct((8, 128), F32),
        ],
        in_specs=[anywhere] * 10,
        out_specs=[anywhere] * 8,
        scratch_shapes=[
            pltpu.SMEM((1, 8), jnp.int32),
            vmem((1, COLS), jnp.int32),
            vmem((8, 128), F32),
            pltpu.SMEM((32,), F32),
            vmem((2, 8, 128), F32),
            vmem((COLS, HEAD), BF16),
            vmem((PAD + COLS, HEAD), BF16),
            vmem((PAD + COLS, HEAD), BF16),
            vmem((COLS + PAD, HEAD), BF16),
            vmem((CTX, ROWS, HEAD), BF16),
            vmem((ROWS, COLS), BF16),
            vmem((ROWS, COLS), BF16),
            vmem((ROWS, COLS), BF16),
            vmem((ROWS, COLS), BF16),
            vmem((ROWS, COLS), BF16),
            vmem((ROWS, COLS), F32),
            vmem((NX, NYL, NZ * WROWS, COLS), BF16),
            vmem((1, PAD + COLS), jnp.int32),
            vmem((ROWS, SLAB), F32),
            vmem((CTX, ROWS, SLAB), F32),
            vmem((CTX, ROWS, SLAB), jnp.int32),
            vmem((CTX, ROWS, SLAB), BF16),
            vmem((CTX + 4, ROWS, SLAB), BF16),
            vmem((HEAD, COLS), BF16),
            vmem((HEAD, PAD + COLS), F32),
            vmem((3, CTX, ROWS, HEAD), BF16),
            vmem((ROWS, 768), F32),
            vmem((ROWS, COLS), BF16),
            vmem((ROWS, COLS), BF16),
            vmem((NX, NYL, 128, 512), BF16),
            vmem((NX, NYL, 128, 512), F32),
            vmem((NX, NYL, 128, 512), BF16),
            vmem((NX, NYL, 128, 512), BF16),
            vmem((NX, NYL, 128, 384), BF16),
            vmem((NYL, 128, 384), BF16),
            vmem((NZ, NYL, WROWS, 384), BF16),
            vmem((NZ, NX, NYL, WROWS, 128), BF16),
            vmem((NX, NYL, WROWS, 128), BF16),
            vmem((NX, NYL, WROWS, 128), BF16),
            vmem((NYL, WROWS, 512), F32),
            vmem((NYL * NYH, WROWS, 128), F32),
            vmem((WROWS, 128), F32),
            vmem((WROWS, COLS), F32),
            vmem((3, 8, 128), F32),
            vmem((3, 8, 8, 128), F32),
            dma(18),
            dma(3, 8), dma(3, 8),
            dma(2, 8), dma(2, 8),
            dma(2, 4), dma(2, 4),
            dma(1), dma(1),
            dma(4), dma(4),
            dma(2, 8), dma(2, 8),
            dma(2, 8), dma(2, 8),
            dma(3, 8), dma(3, 8),
            dma(5), dma(5),
            dma(2, 4), dma(2, 4),
            dma(2, 8), dma(2, 8),
            dma(8), dma(8),
            dma(8), dma(8),
            dma(3, 8), dma(3, 8),
        ],
        compiler_params=pltpu.CompilerParams(
            collective_id=0, has_side_effects=True, vmem_limit_bytes=56 * 1024 * 1024
        ),
    )(
        query_in,
        key_in,
        value_in,
        gate_in,
        out_grad,
        out_weight,
        lengths,
        stamps,
        pos_bias.reshape(8, 128),
        time_bias,
    )
    outs = pl.pallas_call(
        hand_over,
        out_shape=[jax.ShapeDtypeStruct(out.shape, out.dtype) for out in outs[:7]]
        + [jax.ShapeDtypeStruct((32,), F32)],
        in_specs=[anywhere] * 7 + [in_vmem],
        out_specs=[anywhere] * 7 + [in_vmem],
        scratch_shapes=[vmem(out.shape, out.dtype) for out in outs[:7]] + [dma(2, 7)],
        compiler_params=pltpu.CompilerParams(vmem_limit_bytes=56 * 1024 * 1024),
    )(*outs)
    layer_out, query_grad, key_grad, value_grad, gate_grad, weight_grad, pos, timed = outs
    return (
        layer_out,
        query_grad,
        key_grad,
        value_grad,
        gate_grad,
        weight_grad,
        pos.reshape(COLS),
        timed,
    )


def solution(mesh):
    rows = P("dp", "ctx", None)
    owned = P("dp", None)
    return jax.shard_map(
        on_device,
        mesh=mesh,
        in_specs=(rows, rows, rows, rows, rows, owned, owned, owned, P(), P()),
        out_specs=(rows, rows, rows, rows, rows, owned, P(), P()),
        check_vma=False,
    )
```

time: 107 us -> 85.8 us (0.80); the launches traced: 106 us -> 85.6 us
  Pallas kernels: 96.8 us -> 85 us
  local copies, waits for them, and re-layouts: 8.16 us -> 0 us
    pallas_call x1, Pallas kernels: 96.8 us -> 81.7 us  [on_device(): pl.pallas_call(kernel, out_shape=[rows_shape] * 5 + [jax.ShapeDtypeStruct...]
    unnamed x19 -> x0, local copies, waits for them, and re-layouts: 6.97 us -> none
    pallas_call x0 -> x1, Pallas kernels: none -> 3.32 us  [on_device(): pl.pallas_call(hand_over, out_shape=[jax.ShapeDtypeStruct(out.shape, out....]
    squeeze x1 -> x0, local copies, waits for them, and re-layouts: 1.19 us -> none  [on_device(): timed[0, :32]]
where the time goes in v2:
time: 85.8 us; the launch traced here: 85.6 us
  Pallas kernels  85 us (99%)
    pallas_call x1, Pallas kernels, on_device(): pl.pallas_call(kernel, out_shape=[rows_shape] * 5 + [jax.ShapeDtypeStruct...  81.7 us
    pallas_call x1, Pallas kernels, on_device(): pl.pallas_call(hand_over, out_shape=[jax.ShapeDtypeStruct(out.shape, out....  3.32 us

profile of v2, /device:TPU:1, one launch (start us, length us, event | category | flops | bytes accessed | tf_op | source)
XLA Modules:
  0.0 85.6 jit_solution(12719165682345892283)
XLA Ops:
  0.6 81.7 %shard_map.161 = (bf16[1,128,1024]{2,1,0:T(8,128)(2,1)}, bf16[1,128,1024]{2,1,0:T(8,128)(2,1)}, bf16[1,128,1024]{2,1,0:T(8,128)(2,1)}, bf16[1,128,1024]{2,1,0:T(...) custom-call(bf16[1,128,1024]{2,1,0:T(8,128)(2,1)} %q_in.1, ...), custom_call_target="tpu_custom_call" | custom-call | tf_op jit(solution)/shard_map/pallas_call | solution.py:667
  82.3 3.3 %shard_map.162 = (bf16[1,128,1024]{2,1,0:T(8,128)(2,1)}, bf16[1,128,1024]{2,1,0:T(8,128)(2,1)}, bf16[1,128,1024]{2,1,0:T(8,128)(2,1)}, bf16[1,128,1024]{2,1,0:T(...) custom-call(bf16[1,128,1024]{2,1,0:T(8,128)(2,1)} %get-tuple-element.24.refs_0_,, ...), custom_call_target="tpu_custom_call" | custom-call | tf_op jit(solution)/shard_map/pallas_call | solution.py:754

commit v3 on v2

--- a/solution.py
+++ b/solution.py
@@ -51,7 +51,7 @@
     len_ref, stamp_ref, pos_ref, time_ref, table_v,
     qh, kh, vh, doh, o_send, o_row, a_send, gate, ograd, mixed, mgrad, wbuf,
     stamp_pad, tz, bias, bucket, wts, wts_t, q_t, dk_t, d_send, pos_fold,
-    lo_v, gg_v, w_send, w_own, w_r0, w_s0, w_ax, w_a1, w_az, w_bz, w_b1, w_bx, w_s2, w_r3, w_s3, w_land,
+    lo_v, gg_v, w_send, w_own, w_r0, w_s0, w_ax, w_a1, w_az, w_bz, w_b1, w_bx, w_s2, w_r3, w_land,
     b_v, b_r,
     loc, qkv_s, qkv_r, wz_s, wz_r, wx_s, wx_r, wy_s, wy_r, wc_s, wc_r,
     o_s, o_r, a_s, a_r, d_s, d_r, rc_s, rc_r, rx_s, rx_r, rz_s, rz_r, ry_s, ry_r,
@@ -157,7 +157,6 @@
         copy.start()
     for k in (3, 4, 5, 2, 6, 1, 7):
         qkv_copy(2, k).start()
-
     kh[0:PAD, :] = jnp.zeros((PAD, HEAD), BF16)
     vh[0:PAD, :] = jnp.zeros((PAD, HEAD), BF16)
     doh[COLS:, :] = jnp.zeros((PAD, HEAD), BF16)
@@ -405,18 +404,6 @@
         where = ctx_peer(k)
         return remote(d_send.at[a, where[1]], outs[a].at[0, :, my_cols], d_s.at[a, k], d_r.at[a, k], where)
 
-    def value_block(i):
-        slab = pl.ds(aligned(i * ROWS), SLAB)
-        d_send[2, i] = dot(wts_t[i + 4], doh[slab, :]).astype(BF16)
-
-    def value_step(k, unused):
-        value_block(lax.rem(me + k, CTX))
-        d_copy(2, k).start()
-        return unused
-
-    lax.fori_loop(1, CTX, value_step, 0)
-    value_block(me)
-
     def query_block(i):
         rows = pl.ds(aligned(i * ROWS), ROWS)
         slab = pl.ds(aligned(i * ROWS), SLAB)
@@ -434,6 +421,17 @@
     lax.fori_loop(1, CTX, query_step, 0)
     query_block(me)
 
+    def key_block(i):
+        rows = pl.ds(aligned(PAD + i * ROWS), ROWS)
+        d_send[1, i] = (jnp.transpose(dk_t[:, rows]) * FACTOR).astype(BF16)
+
+    def key_step(k, unused):
+        key_block(lax.rem(me + k, CTX))
+        d_copy(1, k).start()
+        return unused
+
+    lax.fori_loop(1, CTX, key_step, 0)
+    key_block(me)
     pos_fold[:, 0:128] = jnp.zeros((ROWS, 128), F32)
 
     def slab_sum(n, unused):
@@ -481,6 +479,7 @@
     totals = tuple(jnp.zeros((8, 128), F32) for unused in range(BUCKETS))
     for first, count, blocks in ((0, 1, ()), (1, 1, (3,)), (2, 1, (2, 3)), (3, 1, (1, 2, 3))):
         totals = lax.fori_loop(0, 16 * count, histogram(first, blocks), totals)
+
     for k in range(1, NX):
         ax_copy(k).wait_recv()
 
@@ -518,8 +517,8 @@
         timed = jnp.where(lane8 == b, whole, timed)
     sums = jnp.where(row8 == 4, timed, sums)
 
-    slots = (me, z, x * NYL + yl)
-    b_peers = (ctx_peer, z_peer, xy_peer)
+    slots = (z, x * NYL + yl, me)
+    b_peers = (z_peer, xy_peer, ctx_peer)
 
     def b_copy(level, k):
         return remote(b_v.at[level], b_r.at[level, slots[level]], b_s.at[level, k], b_rs.at[level, k], b_peers[level](k))
@@ -540,17 +539,18 @@
 
     b_start(0, sums)
 
-    def key_block(i):
-        rows = pl.ds(aligned(PAD + i * ROWS), ROWS)
-        d_send[1, i] = (jnp.transpose(dk_t[:, rows]) * FACTOR).astype(BF16)
-
-    def key_step(k, unused):
-        key_block(lax.rem(me + k, CTX))
-        d_copy(1, k).start()
-        return unused
-
-    lax.fori_loop(1, CTX, key_step, 0)
-    key_block(me)
+    def value_block(i):
+        slab = pl.ds(aligned(i * ROWS), SLAB)
+        d_send[2, i] = dot(wts_t[i + 4], doh[slab, :]).astype(BF16)
+
+    def value_step(k, unused):
+        value_block(lax.rem(me + k, CTX))
+        d_copy(2, k).start()
+        return unused
+
+    lax.fori_loop(1, CTX, value_step, 0)
+    value_block(me)
+
     d_own = [
         pltpu.make_async_copy(d_send.at[a, me], outs[a].at[0, :, my_cols], loc.at[8 + a])
         for a in range(3)
@@ -558,47 +558,66 @@
     for copy in d_own:
         copy.start()
 
+    b_start(1, b_finish(0))
+
+    y_slot = yl * NYH + yh
+
     def ry_copy(k):
         to_yl = lax.rem(yl + k // NYH, NYL)
-        cols = pl.ds(aligned(lax.rem(yh + k % NYH, NYH) * 128), 128)
-        return remote(w_s2.at[to_yl, :, cols], w_r3.at[k], ry_s.at[k], ry_r.at[k], y_peer(k))
+        return remote(w_s2.at[to_yl], w_r3.at[y_slot], ry_s.at[k], ry_r.at[k], y_peer(k))
 
     for k in range(1, NZ):
         az_copy(k).wait_recv()
     total = w_a1[:, z_rows(0), :].astype(F32)
     for k in range(1, NZ):
         total = total + w_az[k].astype(F32)
-    w_s2[:, :, wide] = total
+    w_s2[:, :, wide] = total.astype(BF16)
     for k in range(1, NX):
         bx_copy(k).wait_recv()
     total = w_b1[x].astype(F32)
     for k in range(1, NX):
         total = total + w_bx[k].astype(F32)
-    w_s2[:, :, narrow_cols] = total
+    w_s2[:, :, narrow_cols] = total.astype(BF16)
+    w_r3[y_slot] = w_s2[yl]
     for k in range(1, NYL * NYH):
         ry_copy(k).start()
 
-    b_start(1, b_finish(0))
+
+    b_start(2, b_finish(1))
+
+    for k in range(1, CTX):
+        for a in range(3):
+            qkv_copy(a, k).wait_send()
+        for part in range(2):
+            wz_copy(part, k).wait_send()
+            o_copy(part, k).wait_send()
+            a_copy(part, k).wait_send()
+        bz_copy(k).wait_send()
+    for k in range(1, NX):
+        for which in range(2):
+            wx_copy(which, k).wait_send()
+        ax_copy(k).wait_send()
+    for k in range(1, NX + 1):
+        rc_copy(k).wait_send()
+    for k in range(NX):
+        wc_copy(k).wait_send()
+    wy_copy().wait_send()
 
     for k in range(1, NYL * NYH):
         ry_copy(k).wait_recv()
-    piece = w_s2[yl, :, pl.ds(aligned(yh * 128), 128)]
-    for k in range(1, NYL * NYH):
-        piece = piece + w_r3[k]
-    w_s3[...] = piece
-    piece_cols = pl.ds(aligned(core * 512 + yh * 128), 128)
-    w_land[:, piece_cols] = piece
-
-    def ag_copy(k):
-        return remote(w_s3, w_land.at[:, piece_cols], ag_s.at[k], ag_r.at[k], ctx_peer(k))
-
-    for k in range(1, CTX):
-        ag_copy(k).start()
-
-    b_start(2, b_finish(1))
-
-    for k in range(1, CTX):
-        ag_copy(k).wait_recv()
+    piece = w_r3[0].astype(F32)
+    for slot in range(1, NYL * NYH):
+        piece = piece + w_r3[slot].astype(F32)
+    w_land[:, half] = piece
+
+    def ag_copy():
+        part = w_land.at[:, half]
+        return remote(part, part, ag_s.at[0], ag_r.at[0], (dp, yh * 2 + 1 - core))
+
+    ag_copy().start()
+
+
+    ag_copy().wait_recv()
     wg_copy = pltpu.make_async_copy(w_land, wg_out, loc.at[15])
     wg_copy.start()
 
@@ -614,29 +633,15 @@
 
     for k in range(1, CTX):
         for a in range(3):
-            qkv_copy(a, k).wait_send()
             b_copy(a, k).wait_send()
-        for part in range(2):
-            wz_copy(part, k).wait_send()
-            o_copy(part, k).wait_send()
-            a_copy(part, k).wait_send()
         az_copy(k).wait_send()
-        bz_copy(k).wait_send()
         ry_copy(k).wait_send()
-        ag_copy(k).wait_send()
-    for k in range(1, NX):
-        for which in range(2):
-            wx_copy(which, k).wait_send()
-        ax_copy(k).wait_send()
+    for k in range(1, NX):
         bx_copy(k).wait_send()
-    for k in range(1, NX + 1):
-        rc_copy(k).wait_send()
-    for k in range(NX):
-        wc_copy(k).wait_send()
-    wy_copy().wait_send()
+    ag_copy().wait_send()
     for copy in d_own + out_copies + table_copies + [wg_copy]:
         copy.wait()
-    for a in (2, 0, 1):
+    for a in (0, 1, 2):
         for k in range(1, CTX):
             d_copy(a, k).wait_recv()
             d_copy(a, k).wait_send()
@@ -714,9 +719,8 @@
             vmem((NZ, NX, NYL, WROWS, 128), BF16),
             vmem((NX, NYL, WROWS, 128), BF16),
             vmem((NX, NYL, WROWS, 128), BF16),
-            vmem((NYL, WROWS, 512), F32),
-            vmem((NYL * NYH, WROWS, 128), F32),
-            vmem((WROWS, 128), F32),
+            vmem((NYL, WROWS, 512), BF16),
+            vmem((NYL * NYH, WROWS, 512), BF16),
             vmem((WROWS, COLS), F32),
             vmem((3, 8, 128), F32),
             vmem((3, 8, 8, 128), F32),

time: 85.8 us -> 84.8 us (0.988)
  Pallas kernels: 85 us -> 83.9 us
    pallas_call x1, Pallas kernels: 81.7 us -> 80.6 us  [on_device(): pl.pallas_call(kernel, out_shape=[rows_shape] * 5 + [jax.ShapeDtypeStruct...]
where the time goes in v3:
time: 84.8 us; the launch traced here: 84.6 us
  Pallas kernels  83.9 us (99%)
    pallas_call x1, Pallas kernels, on_device(): pl.pallas_call(kernel, out_shape=[rows_shape] * 5 + [jax.ShapeDtypeStruct...  80.6 us
    pallas_call x1, Pallas kernels, on_device(): pl.pallas_call(hand_over, out_shape=[jax.ShapeDtypeStruct(out.shape, out....  3.32 us

profile of v3, /device:TPU:1, one launch (start us, length us, event | category | flops | bytes accessed | tf_op | source)
XLA Modules:
  0.0 84.6 jit_solution(8081727005985288166)
XLA Ops:
  0.6 80.6 %shard_map.161 = (bf16[1,128,1024]{2,1,0:T(8,128)(2,1)}, bf16[1,128,1024]{2,1,0:T(8,128)(2,1)}, bf16[1,128,1024]{2,1,0:T(8,128)(2,1)}, bf16[1,128,1024]{2,1,0:T(...) custom-call(bf16[1,128,1024]{2,1,0:T(8,128)(2,1)} %q_in.1, ...), custom_call_target="tpu_custom_call" | custom-call | tf_op jit(solution)/shard_map/pallas_call | solution.py:672
  81.3 3.3 %shard_map.162 = (bf16[1,128,1024]{2,1,0:T(8,128)(2,1)}, bf16[1,128,1024]{2,1,0:T(8,128)(2,1)}, bf16[1,128,1024]{2,1,0:T(8,128)(2,1)}, bf16[1,128,1024]{2,1,0:T(...) custom-call(bf16[1,128,1024]{2,1,0:T(8,128)(2,1)} %get-tuple-element.24.refs_0_,, ...), custom_call_target="tpu_custom_call" | custom-call | tf_op jit(solution)/shard_map/pallas_call | solution.py:758

commit v4 on v3

--- a/solution.py
+++ b/solution.py
@@ -277,7 +277,7 @@
 
     for k in range(1, CTX):
         qkv_copy(2, k).wait_recv()
-    lax.fori_loop(1, CTX, attend_step, 0)
+    lax.fori_loop(1, CTX, attend_step, 0, unroll=7)
     for k in range(1, CTX):
         o_copy(1, k).start()
     o_row[:, my_cols] = attend(me)
@@ -418,7 +418,7 @@
         d_copy(0, k).start()
         return unused
 
-    lax.fori_loop(1, CTX, query_step, 0)
+    lax.fori_loop(1, CTX, query_step, 0, unroll=7)
     query_block(me)
 
     def key_block(i):

time: 84.8 us -> 84.7 us (level)
  no operation moved by 1% of the time
where the time goes in v4:
time: 84.7 us; the launch traced here: 84.5 us
  Pallas kernels  83.9 us (99%)
    pallas_call x1, Pallas kernels, on_device(): pl.pallas_call(kernel, out_shape=[rows_shape] * 5 + [jax.ShapeDtypeStruct...  80.5 us
    pallas_call x1, Pallas kernels, on_device(): pl.pallas_call(hand_over, out_shape=[jax.ShapeDtypeStruct(out.shape, out....  3.32 us

profile of v4, /device:TPU:1, one launch (start us, length us, event | category | flops | bytes accessed | tf_op | source)
XLA Modules:
  0.0 84.5 jit_solution(5776288649237901059)
XLA Ops:
  0.6 80.5 %shard_map.161 = (bf16[1,128,1024]{2,1,0:T(8,128)(2,1)}, bf16[1,128,1024]{2,1,0:T(8,128)(2,1)}, bf16[1,128,1024]{2,1,0:T(8,128)(2,1)}, bf16[1,128,1024]{2,1,0:T(...) custom-call(bf16[1,128,1024]{2,1,0:T(8,128)(2,1)} %q_in.1, ...), custom_call_target="tpu_custom_call" | custom-call | tf_op jit(solution)/shard_map/pallas_call | solution.py:672
  81.2 3.3 %shard_map.162 = (bf16[1,128,1024]{2,1,0:T(8,128)(2,1)}, bf16[1,128,1024]{2,1,0:T(8,128)(2,1)}, bf16[1,128,1024]{2,1,0:T(8,128)(2,1)}, bf16[1,128,1024]{2,1,0:T(...) custom-call(bf16[1,128,1024]{2,1,0:T(8,128)(2,1)} %get-tuple-element.24.refs_0_,, ...), custom_call_target="tpu_custom_call" | custom-call | tf_op jit(solution)/shard_map/pallas_call | solution.py:758
